TPU v7x, 32 devices: a whole 2x2x4 slice. The times are simulated.
32 devices in a mesh: tiles: 16 (over z, y, x), chan: 2 (over core).
Axes of the slice: x: 2, y: 2, z: 4, core: 2. Of those that a mesh axis runs over, the one named last changes fastest.
Arguments:
- ocean_state: bfloat16 [16, 22, 2, 16, 3072], P('tiles', None, 'chan'), may hold values from -24 to 24
- land_mask: int32 [16, 22], P('tiles'), may hold values from 0 to 1, as said below
- cotangent: bfloat16 [224, 2, 16, 3072], P('tiles', 'chan'), may hold values from -6 to 6
- depth_kernel: float32 [7, 7, 384], P(None, None, 'chan'), may hold values from -1.8 to 1.8
- norm_gain: float32 [384], P('chan'), may hold values from 0.5 to 1.5
- norm_shift: float32 [384], P('chan'), may hold values from -3 to 3
- weight_in: bfloat16 [384, 1536], P(None, 'chan'), may hold values from -0.3125 to 0.3125
- bias_in: float32 [1536], P('chan'), may hold values from -3 to 3
- weight_out: bfloat16 [1536, 384], P('chan'), may hold values from -0.15625 to 0.15625
- bias_out: float32 [384], P('chan'), may hold values from -3 to 3
- layer_scale: float32 [384], P('chan'), may hold values from 0.3 to 1
Outputs:
- block_out: bfloat16 [224, 2, 16, 3072], P('tiles', 'chan')
- grad_state: bfloat16 [16, 22, 2, 16, 3072], P('tiles', None, 'chan')
- grad_kernel: float32 [7, 7, 384], P(None, None, 'chan')
- grad_gain: float32 [384], P('chan')
- grad_shift: float32 [384], P('chan')
- grad_weight_in: float32 [384, 1536], P(None, 'chan')
- grad_bias_in: float32 [1536], P('chan')
- grad_weight_out: float32 [1536, 384], P('chan')
- grad_bias_out: float32 [384], P('chan')
- grad_scale: float32 [384], P('chan')
Inputs may be any that keep to these rules, and one draw needn't show every extreme that they name: `land_mask`: exactly 224 entries are 1, and some band is ocean in all its 22 slots.
All inputs are finite; a program needn't handle non-finite values.
Results may differ from a plain program's by a relative error of at most 0.014.
Values may be sent and summed in bfloat16 or wider, within the bound.
A program may use at most 128 MiB of HBM per device.

v0:
```python
import jax
import jax.numpy as jnp
from jax import lax
from jax.sharding import PartitionSpec as P

EPS = 1e-06
ROOT_TWO_PI = 0.7978845608028654
CUBIC = 0.044715


def extended(block, sides, width):
    for axis, dim in sides:
        count = lax.axis_size(axis)
        forward = [(i, i + 1) for i in range(count - 1)]
        backward = [(target, source) for source, target in forward]
        low = lax.ppermute(
            lax.slice_in_dim(block, block.shape[dim] - width, None, axis=dim), axis, forward
        )
        high = lax.ppermute(lax.slice_in_dim(block, 0, width, axis=dim), axis, backward)
        block = jnp.concatenate([low, block, high], axis=dim)
    return block


def entering(value, axis, join, neutral):
    count, mine = (lax.axis_size(axis), lax.axis_index(axis))
    pieces = lax.all_gather(value, axis)
    subtotal = jnp.full_like(value, 0) + jnp.asarray(neutral, value.dtype)

    def hop(position, subtotal):
        longer = join(subtotal, pieces[position])
        return jnp.where(position < mine, longer, subtotal)

    return lax.fori_loop(0, count - 1, hop, subtotal)


def gelu_pair(values):
    inner_arg = ROOT_TWO_PI * (values + CUBIC * values * values * values)
    tangent = jnp.tanh(inner_arg)
    gelu_value = 0.5 * values * (1.0 + tangent)
    gelu_slope = 0.5 * (1.0 + tangent) + 0.5 * values * (1.0 - tangent * tangent) * ROOT_TWO_PI * (
        1.0 + 3.0 * CUBIC * values * values
    )
    return (gelu_value, gelu_slope)


def rounded(values):
    return lax.optimization_barrier(values.astype(jnp.bfloat16)).astype(jnp.float32)


def depthwise(padded, kernel, out_side):
    kernel_span = kernel.shape[0]
    accumulated = jnp.zeros((padded.shape[0], out_side, out_side, padded.shape[3]), jnp.float32)
    for down_step in range(kernel_span):
        for east_step in range(kernel_span):
            window = padded[
                :, down_step : down_step + out_side, east_step : east_step + out_side, :
            ]
            accumulated = accumulated + window.astype(jnp.float32) * kernel[down_step, east_step]
    return accumulated


def spread_back(back_tiles, kernel, out_side):
    reach_cells = kernel.shape[0] - 1
    widened = jnp.pad(
        back_tiles, ((0, 0), (reach_cells, reach_cells), (reach_cells, reach_cells), (0, 0))
    )
    return depthwise(widened, kernel[::-1, ::-1], out_side)


def kernel_grads(back_tiles, framed, tile_side, kernel_span):
    back_float = back_tiles.astype(jnp.float32)
    rows_out = []
    for down_step in range(kernel_span):
        kernel_row = []
        for east_step in range(kernel_span):
            window = framed[
                :, down_step : down_step + tile_side, east_step : east_step + tile_side, :
            ].astype(jnp.float32)
            kernel_row.append(jnp.sum(back_float * window, axis=(0, 1, 2)))
        rows_out.append(jnp.stack(kernel_row))
    return jnp.stack(rows_out)


def add_counts(earlier, later):
    return earlier + later


def on_device(
    ocean_state,
    land_mask,
    cotangent,
    depth_kernel,
    norm_gain,
    norm_shift,
    weight_in,
    bias_in,
    weight_out,
    bias_out,
    layer_scale,
):
    device_count = lax.axis_size("tiles")
    ocean_flags = land_mask[0]
    slot_count = ocean_flags.shape[0]
    tile_side = ocean_state.shape[3]
    local_chans = ocean_state.shape[4] // tile_side
    state_cells = ocean_state[0, :, 0].reshape(slot_count, tile_side, tile_side, local_chans)
    kernel_span = depth_kernel.shape[0]
    margin = kernel_span // 2
    padded_side = tile_side + 2 * margin
    capacity = -(-slot_count // device_count)
    buffer_slots = device_count * capacity
    tile_count = cotangent.shape[0]
    cotangent_cells = cotangent[:, 0].reshape(tile_count, tile_side, tile_side, local_chans)
    cell_count = tile_count * tile_side * tile_side
    chans_total = lax.axis_size("chan") * local_chans
    flag_tiles = ocean_flags.astype(jnp.bfloat16)[:, None, None, None]
    masked = state_cells * flag_tiles
    with_rows = extended(masked, (("tiles", 1),), margin)
    west_edge = jnp.roll(with_rows, 1, axis=0)[:, :, tile_side - margin :, :]
    east_edge = jnp.roll(with_rows, -1, axis=0)[:, :, :margin, :]
    framed = jnp.concatenate([west_edge, with_rows, east_edge], axis=2)
    ocean_count = jnp.sum(ocean_flags)
    offset = entering(
        jnp.reshape(ocean_count, (1,)), "tiles", add_counts, jnp.zeros((1,), jnp.int32)
    )[0]
    inclusive = jnp.cumsum(ocean_flags)
    buffer_index = jnp.arange(buffer_slots, dtype=jnp.int32)
    target = buffer_index // capacity
    slot_depth = buffer_index % capacity
    local_rank = slot_depth * device_count + (target - offset) % device_count
    carried = local_rank < ocean_count
    source_slot = jnp.sum((inclusive[None, :] <= local_rank[:, None]).astype(jnp.int32), axis=1)
    source_slot = jnp.minimum(source_slot, slot_count - 1)
    outgoing = (
        jnp.take(framed, source_slot, axis=0) * carried.astype(jnp.bfloat16)[:, None, None, None]
    )
    outgoing = outgoing.reshape((device_count, capacity) + framed.shape[1:])
    sent_flags = carried.astype(jnp.int32).reshape(device_count, capacity)
    arrived, arrived_flags = (
        lax.all_to_all(outgoing, "tiles", split_axis=0, concat_axis=0, tiled=True),
        lax.all_to_all(sent_flags, "tiles", split_axis=0, concat_axis=0, tiled=True),
    )
    arrived = arrived.reshape((buffer_slots,) + framed.shape[1:])
    arrived_flags = arrived_flags.reshape(buffer_slots)
    arrived_rank = jnp.cumsum(arrived_flags).astype(jnp.int32)
    list_slots = jnp.arange(tile_count, dtype=jnp.int32)
    pick_index = jnp.sum((arrived_rank[None, :] <= list_slots[:, None]).astype(jnp.int32), axis=1)
    pick_index = jnp.minimum(pick_index, buffer_slots - 1)
    tiles_framed = jnp.take(arrived, pick_index, axis=0)
    mixed_field = depthwise(tiles_framed, depth_kernel, tile_side).reshape(cell_count, local_chans)
    sum_first, sum_second = lax.psum(
        (jnp.sum(mixed_field, axis=1), jnp.sum(mixed_field * mixed_field, axis=1)), "chan"
    )
    cell_mean = sum_first / chans_total
    variance = sum_second / chans_total - cell_mean * cell_mean
    norm_factor = lax.rsqrt(variance + EPS)
    normed = (mixed_field - cell_mean[:, None]) * norm_factor[:, None]
    features = (normed * norm_gain + norm_shift).astype(jnp.bfloat16)
    features_all = lax.all_gather(features, "chan", axis=1, tiled=True)
    hidden = jnp.dot(features_all, weight_in, preferred_element_type=jnp.float32) + bias_in
    active, active_slope = gelu_pair(hidden)
    active = active.astype(jnp.bfloat16)
    partial_out = rounded(jnp.dot(active, weight_out, preferred_element_type=jnp.float32))
    branch = (
        lax.psum_scatter(
            partial_out.astype(jnp.bfloat16), "chan", scatter_dimension=1, tiled=True
        ).astype(jnp.float32)
        + bias_out
    )
    centre = tiles_framed[:, margin : margin + tile_side, margin : margin + tile_side, :]
    residual = centre.astype(jnp.float32).reshape(cell_count, local_chans)
    block_out = (
        (residual + layer_scale * branch)
        .astype(jnp.bfloat16)
        .reshape(tile_count, 1, tile_side, tile_side * local_chans)
    )
    upstream = cotangent_cells.astype(jnp.float32).reshape(cell_count, local_chans)
    scaled = layer_scale * upstream
    scaled_bf = scaled.astype(jnp.bfloat16)
    grad_scale = jnp.sum(upstream * branch, axis=0)
    grad_bias_out = jnp.sum(scaled, axis=0)
    scaled_all = lax.all_gather(scaled_bf, "chan", axis=1, tiled=True)
    grad_weight_out = jnp.dot(active.T, scaled_all, preferred_element_type=jnp.float32)
    back_hidden = (
        jnp.dot(scaled_all, weight_out.T, preferred_element_type=jnp.float32) * active_slope
    )
    back_hidden_bf = back_hidden.astype(jnp.bfloat16)
    grad_weight_in = jnp.dot(features_all.T, back_hidden_bf, preferred_element_type=jnp.float32)
    grad_bias_in = jnp.sum(back_hidden, axis=0)
    partial_back = rounded(jnp.dot(back_hidden_bf, weight_in.T, preferred_element_type=jnp.float32))
    back_features = lax.psum_scatter(
        partial_back.astype(jnp.bfloat16), "chan", scatter_dimension=1, tiled=True
    ).astype(jnp.float32)
    back_normed = back_features * norm_gain
    grad_gain = jnp.sum(back_features * normed, axis=0)
    grad_shift = jnp.sum(back_features, axis=0)
    first_sum, second_sum = lax.psum(
        (jnp.sum(back_normed, axis=1), jnp.sum(back_normed * normed, axis=1)), "chan"
    )
    back_mixed = norm_factor[:, None] * (
        back_normed
        - first_sum[:, None] / chans_total
        - normed * (second_sum[:, None] / chans_total)
    )
    back_tiles = back_mixed.astype(jnp.bfloat16).reshape(
        tile_count, tile_side, tile_side, local_chans
    )
    grad_kernel = kernel_grads(back_tiles, tiles_framed, tile_side, kernel_span)
    summed = lax.psum(
        (
            grad_kernel,
            grad_gain,
            grad_shift,
            grad_weight_in,
            grad_bias_in,
            grad_weight_out,
            grad_bias_out,
            grad_scale,
        ),
        "tiles",
    )
    norm_cells = float(device_count * cell_count) ** 0.5
    scaled_sums = [summand / norm_cells for summand in summed]
    send_rank = jnp.maximum(arrived_rank - 1, 0)
    send_valid = arrived_flags.astype(jnp.bfloat16)[:, None, None, None]
    slot_rank = jnp.maximum(inclusive - 1, 0)
    home_index = (offset + slot_rank) % device_count * capacity + slot_rank // device_count
    spread_terms = spread_back(back_tiles, depth_kernel, padded_side).astype(jnp.bfloat16)
    outgoing_back = (jnp.take(spread_terms, send_rank, axis=0) * send_valid).reshape(
        (device_count, capacity) + spread_terms.shape[1:]
    )
    homing = lax.all_to_all(
        outgoing_back, "tiles", split_axis=0, concat_axis=0, tiled=True
    ).reshape((buffer_slots,) + spread_terms.shape[1:])
    slot_terms = jnp.take(homing, home_index, axis=0) * flag_tiles
    rim_rows = jnp.concatenate(
        [slot_terms[:, :margin], slot_terms[:, margin + tile_side :]], axis=1
    )
    with_rims = extended(rim_rows, (("tiles", 1),), margin)
    from_north = with_rims[:, :margin].astype(jnp.float32)
    from_south = with_rims[:, 3 * margin :].astype(jnp.float32)
    body_rows = slot_terms[:, margin : margin + tile_side].astype(jnp.float32)
    body_rows = body_rows + jnp.pad(from_north, ((0, 0), (0, tile_side - margin), (0, 0), (0, 0)))
    body_rows = body_rows + jnp.pad(from_south, ((0, 0), (tile_side - margin, 0), (0, 0), (0, 0)))
    middle = body_rows[:, :, margin : margin + tile_side]
    west_part = jnp.roll(body_rows[:, :, :margin], -1, axis=0)
    east_part = jnp.roll(body_rows[:, :, margin + tile_side :], 1, axis=0)
    summed_terms = middle + jnp.pad(west_part, ((0, 0), (0, 0), (tile_side - margin, 0), (0, 0)))
    summed_terms = summed_terms + jnp.pad(
        east_part, ((0, 0), (0, 0), (0, tile_side - margin), (0, 0))
    )
    grad_cells = (summed_terms * ocean_flags.astype(jnp.float32)[:, None, None, None]).astype(
        jnp.bfloat16
    )
    grad_state = grad_cells.reshape(slot_count, tile_side, tile_side * local_chans)[None, :, None]
    return (
        block_out,
        grad_state,
        scaled_sums[0],
        scaled_sums[1],
        scaled_sums[2],
        scaled_sums[3],
        scaled_sums[4],
        scaled_sums[5],
        scaled_sums[6],
        scaled_sums[7],
    )


def solution(mesh):
    in_specs = (
        P("tiles", None, "chan", None, None),
        P("tiles", None),
        P("tiles", "chan", None, None),
        P(None, None, "chan"),
        P("chan"),
        P("chan"),
        P(None, "chan"),
        P("chan"),
        P("chan", None),
        P("chan"),
        P("chan"),
    )
    out_specs = (
        P("tiles", "chan", None, None),
        P("tiles", None, "chan", None, None),
        P(None, None, "chan"),
        P("chan"),
        P("chan"),
        P(None, "chan"),
        P("chan"),
        P("chan", None),
        P("chan"),
        P("chan"),
    )
    return jax.shard_map(
        on_device, mesh=mesh, in_specs=in_specs, out_specs=out_specs, check_vma=False
    )
```

profile of v0, /device:TPU:0, one launch (start us, length us, event | category | flops | bytes accessed | tf_op | source)
XLA Modules:
  0.0 879.8 jit_solution(6373585010494313586)
XLA Ops:
  9.1 6.0 reshape_squeeze.4
  27.2 31.6 %all-reduce.5 = s32[16]{0:T(128)S(1)} all-reduce(s32[16]{0:T(128)S(1)} %dynamic-update-slice), channel_id=1, replica_groups=mesh['tiles'=16,'chan'=2] {'tiles'}, use_global_device_ids=true, to_apply=%add.5 | all-reduce | flops 16 | bytes 128
  58.8 18.8 %while.13 = (s32[]{:T(128)}, s32[1]{0:T(128)}, s32[]{:T(128)}, s32[16,1]{0,1:T(1,128)S(1)}, s32[]{:T(128)}) while((s32[]{:T(128)}, s32[1]{0:T(128)}, s32[]{:T(128)}, s32[16,1]{0,1:T(1,128)S(1)}, s32[]{:T(128)}) %tuple.168), condition=%wide.region_2.3_spmd, body=%wide.region_1.2_spmd.sunk | while | flops 5 | bytes 107 | solution.py:33
  87.3 11.4 %fusion.8 = bf16[22,22,22,192]{3,2,1,0:T(8,128)(2,1)} fusion(bf16[21,22,16,192]{3,2,1,0:T(8,128)(2,1)S(1)} %get-tuple-element.249, bf16[22,3,16,192]{3,2,1,0:T(8,128)(2,1)} %collective-permute-done.1, bf16[22,16,16,192]{3,2,1,0:T(8,128)(2,1)S(1)} %broadcast_multiply_fusion, bf16[22,3,16,192]{3,2,1,0:T(8,128)(2,1)} %collective-permute-done, ...), kind=kLoop, calls=%fused_computation.119 | loop fusion | flops 44977152 | bytes 12739584 | tf_op jit(solution)/shard_map/concatenate | solution.py:121
  98.8 7.6 gather_fusion
  106.4 12.8 %fusion.6 = bf16[16,2,22,22,192]{4,1,0,3,2:T(2,128)(2,1)S(1)} fusion(pred[16,2]{1,0:T(8,128)(4,1)S(1)} %compare_and_fusion, bf16[16,2,22,22,192]{4,3,2,1,0:T(8,128)(2,1)} %bitcast.184, bf16[16,2]{1,0:T(8,128)(2,1)S(1)} %fusion.145), kind=kLoop, calls=%fused_computation.115 | loop fusion | flops 5947392 | bytes 11894880 | tf_op jit(solution)/shard_map/mul | solution.py:135
  119.3 9.4 %copy.110 = bf16[16,2,22,22,192]{4,1,3,2,0:T(2,128)(2,1)} copy(bf16[16,2,22,22,192]{4,1,0,3,2:T(2,128)(2,1)S(1)} %fusion.6) | data formatting | bytes 11894784 | tf_op jit(solution)/shard_map/mul | solution.py:135
  128.7 7.2 all-to-all-start.1
  138.9 138.8 %all-to-all-done.1 = bf16[16,2,22,22,192]{4,1,3,2,0:T(2,128)(2,1)} async-done(((bf16[16,2,22,22,192]{4,1,3,2,0:T(2,128)(2,1)}), bf16[16,2,22,22,192]{4,1,3,2,0:T(2,128)(2,1)}, u32[]{:S(2)}, u32[]{:S(2)}) %all-to-all-start.1) | async-done | bytes 5947424 | tf_op jit(solution)/shard_map/all_to_all | solution.py:140
  277.8 8.0 copy.124
  285.7 6.1 gather_fusion.1
  294.7 29.1 %fusion.155 = (f32[14,16,16]{2,1,0:T(8,128)S(1)}, f32[14,16,16]{2,1,0:T(8,128)S(1)}, f32[14,16,16,192]{3,2,1,0:T(8,128)}) fusion(f32[192]{0:T(256)S(1)} %bitcast.212, bf16[14,22,22,192]{3,2,1,0:T(8,128)(2,1)S(1)} %broadcast_select_fusion.2, f32[192]{0:T(256)S(1)} %bitcast.214, f32[192]{0:T(256)S(1)} %bitcast.218, f32[192]{0:T(256)S(1)} %bitcast.220, ...), kind=kLoop, calls=%fused_computation.416 | loop fusion | flops 102523904 | bytes 70255360 | tf_op jit(solution)/shard_map/reduce_sum | solution.py:152
  333.4 40.8 %all-gather.3.cloned.1.call-done = bf16[3584,384]{0,1:T(8,128)(2,1)} async-done(((bf16[3584,192]{0,1:T(8,128)(2,1)}), bf16[3584,384]{0,1:T(8,128)(2,1)}) %all-gather.3.cloned.1.call-update) | async-done | bytes 2752528 | tf_op jit(solution)/shard_map/all_gather | solution.py:159
  374.2 10.3 %multiply_convert_fusion = (bf16[3584,768]{1,0:T(8,128)(2,1)S(1)}, f32[3584,768]{1,0:T(8,128)}) fusion(f32[768]{0:T(1024)S(1)} %copy-done.80, bf16[3584,384]{0,1:T(8,128)(2,1)} %all-gather.3.cloned.1.call-done, bf16[384,768]{1,0:T(8,128)(2,1)S(1)} %copy-done), kind=kOutput, calls=%fused_computation.113 | convolution fusion | flops 2141454336 | bytes 19860480 | tf_op jit(solution)/shard_map/dot_general | solution.py:160
  408.5 6.8 multiply_reduce_fusion
  419.2 12.9 %all-gather.5.cloned.1.call-done = bf16[3584,384]{0,1:T(8,128)(2,1)} async-done(((bf16[3584,192]{0,1:T(8,128)(2,1)}), bf16[3584,384]{0,1:T(8,128)(2,1)}) %all-gather.5.cloned.1.call-update) | async-done | bytes 2752528 | tf_op jit(solution)/shard_map/all_gather | solution.py:182
  432.1 12.1 %fusion.165 = (f32[768]{0:T(1024)}, bf16[3584,768]{1,0:T(8,128)(2,1)S(1)}) fusion(f32[3584,768]{1,0:T(8,128)} %get-tuple-element.311, f32[768]{0:T(1024)S(1)} %copy-done.80, bf16[3584,384]{0,1:T(8,128)(2,1)} %all-gather.5.cloned.1.call-done, bf16[768,384]{1,0:T(8,128)(2,1)S(1)} %copy-done.79), kind=kOutput, calls=%fused_computation.425 | convolution fusion | flops 2171731200 | bytes 19863552 | tf_op jit(solution)/shard_map/dot_general | solution.py:185
  453.4 7.6 fusion.166
  476.2 5.7 fusion.67
  482.2 53.2 %add_convert_fusion = bf16[14,22,22,192]{3,2,1,0:T(8,128)(2,1)} fusion(bf16[14,16,16,192]{3,2,1,0:T(8,128)(2,1)S(1)} %bitcast.180, f32[192]{0:T(256)S(1)} %bitcast.217, f32[192]{0:T(256)S(1)} %bitcast.255, f32[192]{0:T(256)S(1)} %bitcast.195, f32[192]{0:T(256)S(1)} %bitcast.211, f32[192]{0:T(256)S(1)} %bitcast.209, f32[192]{0:T(256)S(1)} %bitcast.207, ...), kind=kLoop, calls=%fused_computation.117 | loop fusion | flops 191245824 | bytes 4015872 | tf_op jit(solution)/shard_map/convert_element_type | solution.py:228
  535.3 7.3 gather_fusion.2
  542.7 12.9 %fusion.7 = bf16[16,2,22,22,192]{4,1,0,3,2:T(2,128)(2,1)S(1)} fusion(pred[16,2]{1,0:T(8,128)(4,1)S(1)} %le.82, bf16[16,2,22,22,192]{4,3,2,1,0:T(8,128)(2,1)} %bitcast.185, bf16[16,2]{1,0:T(8,128)(2,1)S(1)} %copy.117), kind=kLoop, calls=%fused_computation.116 | loop fusion | flops 5947392 | bytes 11894880 | tf_op jit(solution)/shard_map/mul | solution.py:229
  555.5 9.4 %copy.118 = bf16[16,2,22,22,192]{4,1,3,2,0:T(2,128)(2,1)} copy(bf16[16,2,22,22,192]{4,1,0,3,2:T(2,128)(2,1)S(1)} %fusion.7) | data formatting | bytes 11894784 | tf_op jit(solution)/shard_map/mul | solution.py:229
  565.0 7.2 all-to-all-start.2
  576.5 72.3 %all-reduce.12.cloned.1.call-done = (f32[384,768]{1,0:T(8,128)}, f32[768,384]{1,0:T(8,128)}) async-done(((f32[384,768]{1,0:T(8,128)}, f32[768,384]{1,0:T(8,128)}), (f32[384,768]{1,0:T(8,128)}, f32[768,384]{1,0:T(8,128)})) %all-reduce.12.cloned.1.call-update) | async-done | bytes 2359312 | tf_op jit(solution)/shard_map/psum | solution.py:209
  653.7 7.8 fusion.116
  661.5 11.5 %fusion.118 = (f32[192]{0:T(256)S(1)}, f32[192]{0:T(256)S(1)}, f32[192]{0:T(256)S(1)}, f32[192]{0:T(256)S(1)}, f32[192]{0:T(256)S(1)}, /*index=5*/f32[192]{0:T(2...) fusion(bf16[14,16,16,192]{3,2,1,0:T(8,128)(2,1)S(1)} %bitcast.1, ...), kind=kLoop, calls=%fused_computation.294 | loop fusion | flops 37843584 | bytes 26162688 | tf_op jit(solution)/shard_map/reduce_sum | solution.py:79
  673.1 11.5 %fusion.117 = (f32[192]{0:T(256)S(1)}, f32[192]{0:T(256)S(1)}, f32[192]{0:T(256)S(1)}, f32[192]{0:T(256)S(1)}, f32[192]{0:T(256)S(1)}, /*index=5*/f32[192]{0:T(2...) fusion(bf16[14,16,16,192]{3,2,1,0:T(8,128)(2,1)S(1)} %bitcast.1, ...), kind=kLoop, calls=%fused_computation.293 | loop fusion | flops 37843584 | bytes 26162688 | tf_op jit(solution)/shard_map/reduce_sum | solution.py:79
  684.9 135.1 %all-reduce.6 = (f32[7,7,192]{2,1,0:T(8,128)S(1)}, f32[192]{0:T(256)S(1)}, f32[192]{0:T(256)S(1)}, f32[768]{0:T(1024)S(1)}, f32[192]{0:T(256)S(1)}, /*index=5*/f32[192]{0:T(256)S(1)}) all-reduce(f32[7,7,192]{2,1,0:T(8,128)S(1)} %constant_dynamic-update-slice_fusion, ...), channel_id=1, replica_groups=mesh['tiles'=16,'chan'=2] {'tiles'}, use_global_device_ids=true, to_apply=%region_66.67 | all-reduce | flops 10944 | bytes 87552 | tf_op jit(solution)/shard_map/psum | solution.py:209
  821.7 8.0 copy.126
  829.7 7.9 gather_fusion.3
  846.8 17.2 %collective-permute-done.2 = bf16[22,3,22,192]{3,2,1,0:T(8,128)(2,1)S(1)} collective-permute-done((bf16[22,3,22,192]{3,2,1,0:T(8,128)(2,1)S(1)}, bf16[22,3,22,192]{3,2,1,0:T(8,128)(2,1)S(1)}, u32[]{:S(2)}, u32[]{:S(2)}) %collective-permute-start.2) | collective-permute-done | bytes 557600 | tf_op jit(solution)/shard_map/ppermute | solution.py:16
  (301 shorter events, 128.1 us)
Async XLA Ops:
  7.2 367.0 %copy-start = (bf16[384,768]{1,0:T(8,128)(2,1)S(1)}, bf16[384,768]{1,0:T(8,128)(2,1)}, u32[]{:S(2)}) copy-start(bf16[384,768]{1,0:T(8,128)(2,1)} %param.19) | copy-start | bytes 1769476
  18.2 66.7 %collective-permute-start = (bf16[22,3,16,192]{3,2,1,0:T(8,128)(2,1)}, bf16[22,3,16,192]{3,2,1,0:T(8,128)(2,1)}, u32[]{:S(2)}, u32[]{:S(2)}) collective-permute-start(bf16[22,3,16,192]{3,2,1,0:T(8,128)(2,1)} %get-tuple-element.251), channel_id=1, source_target_pairs={{0,2},{2,4},{4,6},{6,8},{8,10},{10,12},{12,14},{14,16},{16,18},{18... | collective-permute-start | bytes 1216520 | tf_op jit(solution)/shard_map/ppermute | solution.py:16
  23.9 61.0 %collective-permute-start.1 = (bf16[22,3,16,192]{3,2,1,0:T(8,128)(2,1)}, bf16[22,3,16,192]{3,2,1,0:T(8,128)(2,1)}, u32[]{:S(2)}, u32[]{:S(2)}) collective-permute-start(bf16[22,3,16,192]{3,2,1,0:T(8,128)(2,1)} %get-tuple-element.252), channel_id=1, source_target_pairs={{2,0},{4,2},{6,4},{8,6},{10,8},{12,10},{14,12},{16,14},{18,16},{20... | collective-permute-start | bytes 1216520 | tf_op jit(solution)/shard_map/ppermute | solution.py:19
  79.0 49.7 %all-to-all-start = ((s32[16,1,2]{2,1,0:T(1,128)}), s32[16,1,2]{2,1,0:T(1,128)S(1)}, u32[]{:S(2)}, u32[]{:S(2)}) async-start(s32[16,1,2]{2,1,0:T(1,128)} %compare_convert_fusion), calls=%async_computation | async-start | bytes 16384 | tf_op jit(solution)/shard_map/all_to_all | solution.py:141
  128.7 149.1 %all-to-all-start.1 = ((bf16[16,2,22,22,192]{4,1,3,2,0:T(2,128)(2,1)}), bf16[16,2,22,22,192]{4,1,3,2,0:T(2,128)(2,1)}, u32[]{:S(2)}, u32[]{:S(2)}) async-start(bf16[16,2,22,22,192]{4,1,3,2,0:T(2,128)(2,1)} %copy.110), calls=%async_computation.1 | async-start | bytes 15859712 | tf_op jit(solution)/shard_map/all_to_all | solution.py:140
  135.9 238.3 %all-gather.3.cloned.1.call-start = ((), (), s32[]{:S(2)}) async-start(), calls=%async_computation.5 | async-start | bytes 4128768 | tf_op jit(solution)/shard_map/all_gather | solution.py:159
  136.5 157.9 %copy-start.8 = (f32[1,1,192]{2,1,0:T(1,128)}, f32[1,1,192]{2,1,0:T(1,128)S(1)}, u32[]{:S(2)}) copy-start(f32[1,1,192]{2,1,0:T(1,128)S(1)} %get-tuple-element.264) | copy-start | bytes 2308
  136.5 157.9 %copy-start.10 = (f32[1,1,192]{2,1,0:T(1,128)}, f32[1,1,192]{2,1,0:T(1,128)S(1)}, u32[]{:S(2)}) copy-start(f32[1,1,192]{2,1,0:T(1,128)S(1)} %get-tuple-element.265) | copy-start | bytes 2308
  136.5 157.9 %copy-start.12 = (f32[1,1,192]{2,1,0:T(1,128)}, f32[1,1,192]{2,1,0:T(1,128)S(1)}, u32[]{:S(2)}) copy-start(f32[1,1,192]{2,1,0:T(1,128)S(1)} %get-tuple-element.266) | copy-start | bytes 2308
  136.5 157.9 %copy-start.14 = (f32[1,1,192]{2,1,0:T(1,128)}, f32[1,1,192]{2,1,0:T(1,128)S(1)}, u32[]{:S(2)}) copy-start(f32[1,1,192]{2,1,0:T(1,128)S(1)} %get-tuple-element.267) | copy-start | bytes 2308
  136.6 157.9 %copy-start.16 = (f32[1,1,192]{2,1,0:T(1,128)}, f32[1,1,192]{2,1,0:T(1,128)S(1)}, u32[]{:S(2)}) copy-start(f32[1,1,192]{2,1,0:T(1,128)S(1)} %get-tuple-element.268) | copy-start | bytes 2308
  136.6 157.9 %copy-start.18 = (f32[1,1,192]{2,1,0:T(1,128)}, f32[1,1,192]{2,1,0:T(1,128)S(1)}, u32[]{:S(2)}) copy-start(f32[1,1,192]{2,1,0:T(1,128)S(1)} %get-tuple-element.269) | copy-start | bytes 2308
  136.6 157.9 %copy-start.20 = (f32[1,1,192]{2,1,0:T(1,128)}, f32[1,1,192]{2,1,0:T(1,128)S(1)}, u32[]{:S(2)}) copy-start(f32[1,1,192]{2,1,0:T(1,128)S(1)} %get-tuple-element.270) | copy-start | bytes 2308
  136.6 157.9 %copy-start.22 = (f32[1,1,192]{2,1,0:T(1,128)}, f32[1,1,192]{2,1,0:T(1,128)S(1)}, u32[]{:S(2)}) copy-start(f32[1,1,192]{2,1,0:T(1,128)S(1)} %get-tuple-element.271) | copy-start | bytes 2308
  136.6 157.9 %copy-start.24 = (f32[1,1,192]{2,1,0:T(1,128)}, f32[1,1,192]{2,1,0:T(1,128)S(1)}, u32[]{:S(2)}) copy-start(f32[1,1,192]{2,1,0:T(1,128)S(1)} %get-tuple-element.272) | copy-start | bytes 2308
  136.6 157.8 %copy-start.26 = (f32[1,1,192]{2,1,0:T(1,128)}, f32[1,1,192]{2,1,0:T(1,128)S(1)}, u32[]{:S(2)}) copy-start(f32[1,1,192]{2,1,0:T(1,128)S(1)} %get-tuple-element.273) | copy-start | bytes 2308
  136.6 157.8 %copy-start.28 = (f32[1,1,192]{2,1,0:T(1,128)}, f32[1,1,192]{2,1,0:T(1,128)S(1)}, u32[]{:S(2)}) copy-start(f32[1,1,192]{2,1,0:T(1,128)S(1)} %get-tuple-element.274) | copy-start | bytes 2308
  136.7 157.8 %copy-start.30 = (f32[1,1,192]{2,1,0:T(1,128)}, f32[1,1,192]{2,1,0:T(1,128)S(1)}, u32[]{:S(2)}) copy-start(f32[1,1,192]{2,1,0:T(1,128)S(1)} %get-tuple-element.275) | copy-start | bytes 2308
  136.7 157.8 %copy-start.32 = (f32[1,1,192]{2,1,0:T(1,128)}, f32[1,1,192]{2,1,0:T(1,128)S(1)}, u32[]{:S(2)}) copy-start(f32[1,1,192]{2,1,0:T(1,128)S(1)} %get-tuple-element.276) | copy-start | bytes 2308
  136.7 157.8 %copy-start.34 = (f32[1,1,192]{2,1,0:T(1,128)}, f32[1,1,192]{2,1,0:T(1,128)S(1)}, u32[]{:S(2)}) copy-start(f32[1,1,192]{2,1,0:T(1,128)S(1)} %get-tuple-element.277) | copy-start | bytes 2308
  136.7 157.8 %copy-start.36 = (f32[1,1,192]{2,1,0:T(1,128)}, f32[1,1,192]{2,1,0:T(1,128)S(1)}, u32[]{:S(2)}) copy-start(f32[1,1,192]{2,1,0:T(1,128)S(1)} %get-tuple-element.278) | copy-start | bytes 2308
  136.7 157.8 %copy-start.38 = (f32[1,1,192]{2,1,0:T(1,128)}, f32[1,1,192]{2,1,0:T(1,128)S(1)}, u32[]{:S(2)}) copy-start(f32[1,1,192]{2,1,0:T(1,128)S(1)} %get-tuple-element.279) | copy-start | bytes 2308
  136.7 157.8 %copy-start.40 = (f32[1,1,192]{2,1,0:T(1,128)}, f32[1,1,192]{2,1,0:T(1,128)S(1)}, u32[]{:S(2)}) copy-start(f32[1,1,192]{2,1,0:T(1,128)S(1)} %get-tuple-element.280) | copy-start | bytes 2308
  136.7 157.8 %copy-start.42 = (f32[1,1,192]{2,1,0:T(1,128)}, f32[1,1,192]{2,1,0:T(1,128)S(1)}, u32[]{:S(2)}) copy-start(f32[1,1,192]{2,1,0:T(1,128)S(1)} %get-tuple-element.281) | copy-start | bytes 2308
  136.7 157.8 %copy-start.44 = (f32[1,1,192]{2,1,0:T(1,128)}, f32[1,1,192]{2,1,0:T(1,128)S(1)}, u32[]{:S(2)}) copy-start(f32[1,1,192]{2,1,0:T(1,128)S(1)} %get-tuple-element.282) | copy-start | bytes 2308
  333.4 72.4 %reduce-scatter.7.cloned.1.call-start = ((), (), s32[]{:S(2)}) async-start(), calls=%async_computation.7 | async-start | bytes 4128768
  394.1 38.0 %all-gather.5.cloned.1.call-start = ((), (), s32[]{:S(2)}) async-start(), calls=%async_computation.6 | async-start | bytes 4128768 | tf_op jit(solution)/shard_map/all_gather | solution.py:182
  419.2 45.2 %reduce-scatter.9.cloned.1.call-start = ((), (), s32[]{:S(2)}) async-start(), calls=%async_computation.8 | async-start | bytes 4128768
  452.7 196.1 %all-reduce.12.cloned.1.call-start = ((), (), s32[]{:S(2)}) async-start(), calls=%async_computation.9 | async-start | bytes 4718592 | tf_op jit(solution)/shard_map/psum | solution.py:209
  565.0 256.8 %all-to-all-start.2 = ((bf16[16,2,22,22,192]{4,1,3,2,0:T(2,128)(2,1)}), bf16[16,2,22,22,192]{4,1,3,2,0:T(2,128)(2,1)}, u32[]{:S(2)}, u32[]{:S(2)}) async-start(bf16[16,2,22,22,192]{4,1,3,2,0:T(2,128)(2,1)} %copy.118), calls=%async_computation.2 | async-start | bytes 15859712 | tf_op jit(solution)/shard_map/all_to_all | solution.py:232
  841.0 23.0 %collective-permute-start.2 = (bf16[22,3,22,192]{3,2,1,0:T(8,128)(2,1)S(1)}, bf16[22,3,22,192]{3,2,1,0:T(8,128)(2,1)S(1)}, u32[]{:S(2)}, u32[]{:S(2)}) collective-permute-start(bf16[22,3,22,192]{3,2,1,0:T(8,128)(2,1)S(1)} %get-tuple-element.246), channel_id=1, source_target_pairs={{0,2},{2,4},{4,6},{6,8},{8,10},{10,12},{12,14},{14,16},{16,18},{18... | collective-permute-start | bytes 1672712 | tf_op jit(solution)/shard_map/ppermute | solution.py:16
  843.4 21.3 %collective-permute-start.3 = (bf16[22,3,22,192]{3,2,1,0:T(8,128)(2,1)S(1)}, bf16[22,3,22,192]{3,2,1,0:T(8,128)(2,1)S(1)}, u32[]{:S(2)}, u32[]{:S(2)}) collective-permute-start(bf16[22,3,22,192]{3,2,1,0:T(8,128)(2,1)S(1)} %get-tuple-element.247), channel_id=1, source_target_pairs={{2,0},{4,2},{6,4},{8,6},{10,8},{12,10},{14,12},{16,14},{18,16},{20... | collective-permute-start | bytes 1672712 | tf_op jit(solution)/shard_map/ppermute | solution.py:19
  (66 other events, 1968.6 us)
Sparse Core Ops, SparseCore 0:
  333.5 40.6 all-gather.2
  394.2 11.4 reduce-scatter.6
  419.3 12.7 all-gather.4
  452.8 11.4 reduce-scatter.8
  470.4 178.3 all-reduce.11
where the time goes:
time: 887 us; the launch traced here: 880 us
  waiting for transfers between devices  286 us (32%)
  other arithmetic  204 us (23%)
  blocking collectives  174 us (20%)
  local copies, waits for them, and re-layouts  120 us (14%)
  matrix products  40.9 us (5%)
  starting transfers between devices  29.9 us (3%)
  between operations  15.9 us (2%)
  loops' own time  10.1 us (1%)
    all_to_all x1, waiting for transfers between devices, on_device(): lax.all_to_all(outgoing, 'tiles', split_axis=0, concat_axis=0, tiled=True)  139 us
    psum x1, blocking collectives, on_device(): lax.psum((grad_kernel, grad_gain, grad_shift, grad_weight_in, grad_bias_i...  135 us
    psum x1, waiting for transfers between devices, on_device(): lax.psum((grad_kernel, grad_gain, grad_shift, grad_weight_in, grad_bias_i...  72.3 us
    convert_element_type x1, other arithmetic, on_device(): spread_back(back_tiles, depth_kernel, padded_side).astype(jnp.bfloat16)  53.2 us
    all_gather x1, waiting for transfers between devices, on_device(): features_all = lax.all_gather(features, 'chan', axis=1, tiled=True)  40.8 us
    unnamed x1, blocking collectives  31.6 us
    reduce_sum x3, other arithmetic, kernel_grads(): kernel_row.append(jnp.sum(back_float * window, axis=(0, 1, 2)))  30.9 us
    reduce_sum x1, other arithmetic, on_device(): jnp.sum(mixed_field, axis=1)  29.1 us
  transfers between devices with their start and end apart: 12, of which 7 were waited for; matrix products, arithmetic and copies ran while one was open for 25% of the time, Pallas kernels for 0%

commit v1 on v0

v1 whole, which is shorter than its diff:
```python
import jax
import jax.numpy as jnp
from jax import lax
from jax.sharding import PartitionSpec as P

EPS = 1e-06
ROOT_TWO_PI = 0.7978845608028654
CUBIC = 0.044715
SWAP = ((0, 1), (1, 0))


def swapped(value):
    return lax.ppermute(value, "chan", SWAP)


def row_halo(field, width):
    count = lax.axis_size("tiles")
    forward = [(i, i + 1) for i in range(count - 1)]
    backward = [(target, source) for source, target in forward]
    low = lax.ppermute(field[field.shape[0] - width :], "tiles", forward)
    high = lax.ppermute(field[:width], "tiles", backward)
    return jnp.concatenate([low, field, high], axis=0)


def gelu_pair(values):
    inner_arg = ROOT_TWO_PI * (values + CUBIC * values * values * values)
    tangent = jnp.tanh(inner_arg)
    gelu_value = 0.5 * values * (1.0 + tangent)
    gelu_slope = 0.5 * (1.0 + tangent) + 0.5 * values * (1.0 - tangent * tangent) * ROOT_TWO_PI * (
        1.0 + 3.0 * CUBIC * values * values
    )
    return (gelu_value, gelu_slope)


def depthwise(padded, kernel):
    span = kernel.shape[0]
    rows, cols = padded.shape[0] - span + 1, padded.shape[1] - span + 1
    total = jnp.zeros((rows, cols, padded.shape[2]), jnp.float32)
    for down in range(span):
        for east in range(span):
            window = padded[down : down + rows, east : east + cols]
            total = total + window.astype(jnp.float32) * kernel[down, east]
    return total


def kernel_grads(back, framed, span):
    rows, cols = back.shape[:2]
    back_float = back.astype(jnp.float32)
    sums = []
    for down in range(span):
        for east in range(span):
            window = framed[down : down + rows, east : east + cols].astype(jnp.float32)
            sums.append(jnp.sum(back_float * window, axis=(0, 1)))
    return jnp.stack(sums)


def on_device(
    ocean_state,
    land_mask,
    cotangent,
    depth_kernel,
    norm_gain,
    norm_shift,
    weight_in,
    bias_in,
    weight_out,
    bias_out,
    layer_scale,
):
    devices = lax.axis_size("tiles")
    mine, core = lax.axis_index("tiles"), lax.axis_index("chan")
    slots = land_mask.shape[1]
    half = slots // 2
    side = ocean_state.shape[3]
    own = ocean_state.shape[4] // side
    chans = 2 * own
    span = depth_kernel.shape[0]
    margin = span // 2
    listed = cotangent.shape[0]
    width = half * side
    cells = side * width
    group = weight_in.shape[1]
    cap = -(-half // devices)

    masks = lax.all_gather(land_mask[0], "tiles")
    counts = jnp.sum(masks.reshape(2 * devices, half), axis=1)
    ends = jnp.cumsum(counts)
    starts = ends - counts
    home = mine * 2 + core
    my_start = starts[home]
    flags = lax.dynamic_slice(land_mask[0], (core * half,), (half,))
    inclusive = jnp.cumsum(flags)
    lap = jnp.arange(cap, dtype=jnp.int32)

    wanted = (mine - starts)[:, None] % devices + lap * devices
    wanted = jnp.clip((starts[:, None] + wanted) // devices, 0, listed - 1)
    leaving = jnp.take(cotangent[:, 0], wanted.reshape(-1), axis=0)
    landed = lax.all_to_all(leaving, ("tiles", "chan"), 0, 0, tiled=True)

    vectors = jnp.concatenate(
        [depth_kernel.reshape(-1), norm_gain, norm_shift, bias_out, layer_scale, bias_in]
    )
    others = swapped(vectors)

    def both(low, high, lead=()):
        return jnp.concatenate(
            [vectors[low:high].reshape(lead + (-1,)), others[low:high].reshape(lead + (-1,))],
            axis=-1,
        )

    taps = span * span * own
    kernel = both(0, taps, (span, span))
    gain = both(taps, taps + own)
    shift = both(taps + own, taps + 2 * own)
    bias_o = both(taps + 2 * own, taps + 3 * own)
    scale = both(taps + 3 * own, taps + 4 * own)
    bias_h = both(taps + 4 * own, taps + 4 * own + group)
    w_in = jnp.concatenate([weight_in, swapped(weight_in)], axis=1)
    w_in = jnp.where(core == 0, w_in, jnp.concatenate([w_in[own:], w_in[:own]], axis=0))
    w_out = jnp.concatenate([weight_out, swapped(weight_out)], axis=0)
    w_out = jnp.where(
        core == 0, w_out, jnp.concatenate([w_out[:, own:], w_out[:, :own]], axis=1)
    )

    state = ocean_state[0, :, 0].reshape(slots, side, side, own)
    masked = state * land_mask[0].astype(jnp.bfloat16)[:, None, None, None]
    field = masked.transpose(1, 0, 2, 3).reshape(side, slots * side, own)
    tall = row_halo(field, margin)
    tall = jnp.concatenate(
        [tall[:, slots * side - margin :], tall, tall[:, :margin]], axis=1
    )
    shape = (tall.shape[0], width + 2 * margin, own)
    kept = lax.dynamic_slice(tall, (0, core * width, 0), shape)
    given = lax.dynamic_slice(tall, (0, (1 - core) * width, 0), shape)
    framed = jnp.concatenate([kept, swapped(given)], axis=2)

    on_land = jnp.repeat(flags, side)[None, :, None] == 0
    mixed = jnp.where(on_land, 0.0, depthwise(framed, kernel)).reshape(cells, chans)
    cell_mean = jnp.sum(mixed, axis=1) / chans
    variance = jnp.sum(mixed * mixed, axis=1) / chans - cell_mean * cell_mean
    factor = lax.rsqrt(variance + EPS)
    normed = (mixed - cell_mean[:, None]) * factor[:, None]
    features = (normed * gain + shift).astype(jnp.bfloat16)
    hidden = jnp.dot(features, w_in, preferred_element_type=jnp.float32) + bias_h
    active, slope = gelu_pair(hidden)
    active = active.astype(jnp.bfloat16)
    branch = jnp.dot(active, w_out, preferred_element_type=jnp.float32) + bias_o
    residual = framed[margin : margin + side, margin : margin + width]
    residual = residual.astype(jnp.float32).reshape(cells, chans)
    block = (residual + scale * branch).astype(jnp.bfloat16)
    block = block.reshape(side, half, side, 2, own).transpose(1, 3, 0, 2, 4)
    block = block.reshape(half * 2, side, side * own)

    target = jnp.arange(devices, dtype=jnp.int32)
    rank = (target - my_start)[:, None] % devices + lap * devices
    source = jnp.sum((inclusive <= rank[..., None]).astype(jnp.int32), axis=-1)
    source = jnp.minimum(source, half - 1)
    part = (jnp.arange(2, dtype=jnp.int32) + core) % 2
    source = source[:, None, :] * 2 + part[None, :, None]
    leaving = jnp.take(block, source.reshape(-1), axis=0)
    finished = lax.all_to_all(leaving, ("tiles", "chan"), 0, 0, tiled=True)
    ranks = jnp.arange(listed, dtype=jnp.int32) * devices + mine
    owner = jnp.sum((ends[None, :] <= ranks[:, None]).astype(jnp.int32), axis=1)
    owner = jnp.minimum(owner, 2 * devices - 1)
    pick = owner * cap + (ranks - starts[owner]) // devices
    block_out = jnp.take(finished, pick, axis=0)[:, None]

    local = jnp.maximum(inclusive - 1, 0)
    pick = ((my_start + local) % devices)[:, None] * 2 + part
    pick = pick * cap + (local // devices)[:, None]
    upstream = jnp.take(landed, pick.reshape(-1), axis=0)
    upstream = upstream.reshape(half, 2, side, side, own).transpose(2, 0, 3, 1, 4)
    upstream = upstream.reshape(side, width, chans).astype(jnp.float32)
    upstream = jnp.where(on_land, 0.0, upstream).reshape(cells, chans)
    scaled = scale * upstream
    scaled_bf = scaled.astype(jnp.bfloat16)
    grad_scale = jnp.sum(upstream * branch, axis=0)
    grad_bias_out = jnp.sum(scaled, axis=0)
    grad_w_out = jnp.dot(active.T, scaled_bf, preferred_element_type=jnp.float32)
    back_hidden = jnp.dot(scaled_bf, w_out.T, preferred_element_type=jnp.float32) * slope
    back_hidden_bf = back_hidden.astype(jnp.bfloat16)
    grad_w_in = jnp.dot(features.T, back_hidden_bf, preferred_element_type=jnp.float32)
    grad_bias_in = jnp.sum(back_hidden, axis=0)
    back_features = jnp.dot(back_hidden_bf, w_in.T, preferred_element_type=jnp.float32)

    grad_w_in = jnp.where(
        core == 0, grad_w_in, jnp.concatenate([grad_w_in[own:], grad_w_in[:own]], axis=0)
    )
    grad_w_out = jnp.where(
        core == 0,
        grad_w_out,
        jnp.concatenate([grad_w_out[:, own:], grad_w_out[:, :own]], axis=1),
    )
    norm_cells = float(devices * listed * side * side) ** 0.5
    grad_w_in = (grad_w_in[:, :group] + swapped(grad_w_in[:, group:])) / norm_cells
    grad_w_out = (grad_w_out[:group] + swapped(grad_w_out[group:])) / norm_cells
    grad_w_in, grad_w_out = lax.psum((grad_w_in, grad_w_out), "tiles")

    back_normed = back_features * gain
    grad_gain = jnp.sum(back_features * normed, axis=0)
    grad_shift = jnp.sum(back_features, axis=0)
    first = jnp.sum(back_normed, axis=1) / chans
    second = jnp.sum(back_normed * normed, axis=1) / chans
    back_mixed = factor[:, None] * (back_normed - first[:, None] - normed * second[:, None])
    back = back_mixed.astype(jnp.bfloat16).reshape(side, width, chans)

    back_tall = row_halo(back, margin)
    rims = swapped(
        jnp.concatenate([back_tall[:, :margin], back_tall[:, width - margin :]], axis=1)
    )
    rims = jnp.concatenate([rims[..., own:], rims[..., :own]], axis=2)
    back_framed = jnp.concatenate([rims[:, margin:], back_tall, rims[:, :margin]], axis=1)
    grad_field = depthwise(back_framed, kernel[::-1, ::-1])
    grad_field = jnp.where(on_land, 0.0, grad_field).astype(jnp.bfloat16)
    grad_kept, grad_got = grad_field[..., :own], swapped(grad_field[..., own:])
    grad_cells = jnp.where(
        core == 0,
        jnp.concatenate([grad_kept, grad_got], axis=1),
        jnp.concatenate([grad_got, grad_kept], axis=1),
    )
    grad_cells = grad_cells.reshape(side, slots, side, own).transpose(1, 0, 2, 3)
    grad_state = grad_cells.reshape(1, slots, 1, side, side * own)

    grad_kernel = kernel_grads(back, framed, span)
    by_channel = jnp.concatenate(
        [grad_kernel, jnp.stack([grad_gain, grad_shift, grad_bias_out, grad_scale])], axis=0
    )
    keep = jnp.concatenate([by_channel[:, :own].reshape(-1), grad_bias_in[:group]])
    give = jnp.concatenate([by_channel[:, own:].reshape(-1), grad_bias_in[group:]])
    summed = lax.psum(keep + swapped(give), "tiles") / norm_cells
    ends_at = span * span * own
    rows = summed[ends_at : ends_at + 4 * own].reshape(4, own)
    return (
        block_out,
        grad_state,
        summed[:ends_at].reshape(span, span, own),
        rows[0],
        rows[1],
        grad_w_in,
        summed[ends_at + 4 * own :],
        grad_w_out,
        rows[2],
        rows[3],
    )


def solution(mesh):
    in_specs = (
        P("tiles", None, "chan", None, None),
        P("tiles", None),
        P("tiles", "chan", None, None),
        P(None, None, "chan"),
        P("chan"),
        P("chan"),
        P(None, "chan"),
        P("chan"),
        P("chan", None),
        P("chan"),
        P("chan"),
    )
    out_specs = (
        P("tiles", "chan", None, None),
        P("tiles", None, "chan", None, None),
        P(None, None, "chan"),
        P("chan"),
        P("chan"),
        P(None, "chan"),
        P("chan"),
        P("chan", None),
        P("chan"),
        P("chan"),
    )
    return jax.shard_map(
        on_device, mesh=mesh, in_specs=in_specs, out_specs=out_specs, check_vma=False
    )
```

time: 887 us -> 682 us (0.77)
  waiting for transfers between devices: 286 us -> 19.2 us
  other arithmetic: 204 us -> 329 us
  blocking collectives: 174 us -> 127 us
  local copies, waits for them, and re-layouts: 120 us -> 93.9 us
  matrix products: 40.9 us -> 64.9 us
  loops' own time: 10.1 us -> 0 us
    all_to_all x3 -> x2, waiting for transfers between devices: 139 us -> 0.01 us  [the longest x1 0.01 us: on_device(): landed = lax.all_to_all(leaving, ('tiles', 'chan'), 0, 0, tiled=True)]
    reduce_sum x8 -> x11, other arithmetic: 72.2 us -> 201 us  [the longest x1 99.4 us: on_device(): cell_mean = jnp.sum(mixed, axis=1) / chans]
    psum x3 -> x1, blocking collectives: 142 us -> 77.4 us  [on_device(): summed = lax.psum(keep + swapped(give), 'tiles') / norm_cells]
    all_gather x2 -> x0, waiting for transfers between devices: 53.7 us -> none  [the longest x1 40.8 us: on_device(): features_all = lax.all_gather(features, 'chan', axis=1, tiled=True)]
    psum x1, waiting for transfers between devices: 72.3 us -> 19.2 us  [on_device(): grad_w_in, grad_w_out = lax.psum((grad_w_in, grad_w_out), 'tiles')]
    all_gather x0 -> x1, blocking collectives: none -> 49.5 us  [on_device(): masks = lax.all_gather(land_mask[0], 'tiles')]
    unnamed x1 -> x0, blocking collectives: 31.6 us -> none
    mul x4 -> x3, other arithmetic: 31.1 us -> 2.75 us  [the longest x1 2.08 us: on_device(): masked = state * land_mask[0].astype(jnp.bfloat16)[:, None, None, None]]
  transfers between devices with their start and end apart: 12 -> 16, of which waited for: 7 -> 1; matrix products, arithmetic and copies ran while one was open for 25% -> 44% of each run, Pallas kernels for 0% -> 0%
where the time goes in v1:
time: 682 us; the launch traced here: 676 us
  other arithmetic  329 us (48%)
  blocking collectives  127 us (19%)
  local copies, waits for them, and re-layouts  93.9 us (14%)
  matrix products  64.9 us (10%)
  starting transfers between devices  26.3 us (4%)
  waiting for transfers between devices  19.2 us (3%)
  between operations  16 us (2%)
    reduce_sum x1, other arithmetic, on_device(): cell_mean = jnp.sum(mixed, axis=1) / chans  99.4 us
    reduce_sum x6, other arithmetic, kernel_grads(): sums.append(jnp.sum(back_float * window, axis=(0, 1)))  95.2 us
    psum x1, blocking collectives, on_device(): summed = lax.psum(keep + swapped(give), 'tiles') / norm_cells  77.4 us
    convert_element_type x1, other arithmetic, on_device(): grad_field = jnp.where(on_land, 0.0, grad_field).astype(jnp.bfloat16)  58 us
    all_gather x1, blocking collectives, on_device(): masks = lax.all_gather(land_mask[0], 'tiles')  49.5 us
    dot_general x1, matrix products, on_device(): jnp.dot(scaled_bf, w_out.T, preferred_element_type=jnp.float32) * slope  19.4 us
    psum x1, waiting for transfers between devices, on_device(): grad_w_in, grad_w_out = lax.psum((grad_w_in, grad_w_out), 'tiles')  19.2 us
    concatenate x1, other arithmetic, on_device(): jnp.concatenate([tall[:, slots * side - margin:], tall, tall[:, :margin]]...  15.4 us
  transfers between devices with their start and end apart: 16, of which 1 were waited for; matrix products, arithmetic and copies ran while one was open for 44% of the time, Pallas kernels for 0%

profile of v1, /device:TPU:0, one launch (start us, length us, event | category | flops | bytes accessed | tf_op | source)
XLA Modules:
  0.0 676.1 jit_solution(16829266664952852585)
XLA Ops:
  12.8 6.0 reshape_squeeze.3
  23.6 5.8 collective-permute-start
  29.7 49.5 %all-gather = s32[16,1,22]{2,1,0:T(1,128)S(1)} all-gather(s32[1,1,22]{2,1,0:T(1,128)S(1)} %bitcast.111), channel_id=1, replica_groups=mesh['tiles'=16,'chan'=2] {'tiles'}, dimensions={0}, use_global_device_ids=true | all-gather | bytes 1496 | tf_op jit(solution)/shard_map/all_gather | solution.py:85
  89.5 4.1 all-to-all-start.1
  103.6 15.4 %fusion.137 = bf16[22,358,192]{2,1,0:T(8,128)(2,1)S(1)} fusion(bf16[3,352,192]{2,1,0:T(8,128)(2,1)S(1)} %copy.99, bf16[16,352,192]{2,1,0:T(8,128)(2,1)S(1)} %bitcast.98, bf16[3,352,192]{2,1,0:T(8,128)(2,1)} %copy.98), kind=kLoop, calls=%fused_computation.354 | loop fusion | flops 27219456 | bytes 5998080 | tf_op jit(solution)/shard_map/concatenate | solution.py:129
  135.1 99.4 %fusion.237 = (f32[16,176]{1,0:T(8,128)S(1)}, f32[16,176]{1,0:T(8,128)S(1)}, f32[16,176,384]{2,1,0:T(8,128)}) fusion(f32[384]{0:T(512)S(1)} %get-tuple-element.173, bf16[22,182,192]{2,1,0:T(8,128)(2,1)} %collective-permute-done.2, bf16[22,182,192]{2,1,0:T(8,128)(2,1)S(1)} %get-tuple-element.186, f32[384]{0:T(512)} %get-tuple-element.126, ...), kind=kLoop, calls=%fused_computation.619 | loop fusion | flops 321153536 | bytes 7498416 | tf_op jit(solution)/shard_map/reduce_sum | solution.py:139
  235.0 4.8 fusion.146
  242.9 12.8 %multiply_convert_fusion = (bf16[2816,1536]{1,0:T(8,128)(2,1)}, f32[2816,1536]{1,0:T(8,128)}) fusion(f32[1536]{0:T(1024)S(1)} %pad_maximum_fusion.10, bf16[2816,384]{1,0:T(8,128)(2,1)S(1)} %add_convert_fusion, bf16[384,1536]{1,0:T(8,128)(2,1)S(1)} %constant_dynamic-update-slice_fusion, bf16[192,1536]{1,0:T(8,128)(2,1)S(1)} %copy-done.24, ...), kind=kOutput, calls=%fused_computation.63 | convolution fusion | flops 3368091648 | bytes 30480384 | tf_op jit(solution)/shard_map/dot_general | solution.py:144
  259.7 5.0 gather.32
  264.7 5.9 convert_bitcast_fusion
  270.6 7.9 %reshape.705 = f32[2816,384]{1,0:T(8,128)} reshape(f32[16,11,16,2,192]{4,3,2,1,0:T(2,128)} %convert_bitcast_fusion) | data formatting | bytes 8650752 | tf_op jit(solution)/shard_map/convert_element_type | solution.py:173
  278.5 19.4 %fusion.250 = (f32[1536]{0:T(1024)S(1)}, bf16[2816,1536]{1,0:T(8,128)(2,1)S(1)}) fusion(f32[2816,1536]{1,0:T(8,128)} %get-tuple-element.220, f32[1536]{0:T(1024)S(1)} %pad_maximum_fusion.10, bf16[768,384]{0,1:T(8,128)(2,1)} %collective-permute-done.5, bf16[768,384]{0,1:T(8,128)(2,1)} %copy.101, bf16[1536,192]{0,1:T(8,128)(2,1)} %get-tuple-element.200, ...), kind=kOutput, calls=%fused_computation.631 | convolution fusion | flops 3421272576 | bytes 32653568 | tf_op jit(solution)/shard_map/dot_general | solution.py:180
  297.9 5.0 fusion.132
  302.9 7.9 %multiply_reduce_fusion.1 = (f32[384]{0:T(512)S(1)}, f32[2816]{0:T(1024)S(1)}, f32[2816]{0:T(1024)S(1)}, f32[384]{0:T(512)S(1)}, f32[2816,384]{1,0:T(8,128)}) fusion(f32[16,176,384]{2,1,0:T(8,128)S(1)} %bitcast.95, f32[2816]{0:T(1024)S(1)} %add_rsqrt_fusion, f32[2816]{0:T(1024)S(1)} %div.87, f32[384]{0:T(512)S(1)} %get-tuple-element.228, ...), kind=kOutput, calls=%fused_computation.340 | convolution fusion | flops 3334563328 | bytes 19710464 | tf_op jit(solution)/shard_map/dot_general | solution.py:184
  310.9 6.3 fusion.7
  317.3 9.9 %fusion.236 = f32[1536,384]{0,1:T(8,128)} fusion(bf16[2816,1536]{1,0:T(8,128)(2,1)} %get-tuple-element.219, f32[2816,384]{1,0:T(8,128)} %reshape.705, f32[384]{0:T(512)S(1)} %get-tuple-element.226, pred[2816]{0:T(1024)(128)(4,1)S(1)} %copy-done.69), kind=kOutput, calls=%fused_computation.618 | convolution fusion | flops 3325132800 | bytes 15339776 | tf_op jit(solution)/shard_map/dot_general | solution.py:179
  327.2 9.8 %multiply_reduce_fusion = (f32[384]{0:T(512)S(1)}, bf16[2816,384]{1,0:T(8,128)(2,1)}) fusion(f32[2816,384]{1,0:T(8,128)S(1)} %bitcast.105, pred[2816]{0:T(1024)(128)(4,1)S(1)} %copy-done.69, f32[384]{0:T(512)S(1)} %get-tuple-element.226, f32[16,176,384]{2,1,0:T(8,128)} %fusion.146, f32[384]{0:T(512)S(1)} %copy-done.71, ...), kind=kOutput, calls=%fused_computation.339 | convolution fusion | flops 3334766080 | bytes 21830912 | tf_op jit(solution)/shard_map/dot_general | solution.py:147
  340.9 7.7 %fusion.85 = (f32[384]{0:T(512)S(1)}, f32[384]{0:T(512)S(1)}, f32[384]{0:T(512)S(1)}, f32[384]{0:T(512)S(1)}) fusion(bf16[16,176,384]{2,1,0:T(8,128)(2,1)S(1)} %bitcast.85, bf16[22,182,192]{2,1,0:T(8,128)(2,1)} %collective-permute-done.2, bf16[22,182,192]{2,1,0:T(8,128)(2,1)S(1)} %copy-done.4), kind=kLoop, calls=%fused_computation.290 | loop fusion | flops 27032064 | bytes 5243904 | tf_op jit(solution)/shard_map/reduce_sum | solution.py:53
  348.7 17.9 %fusion.125 = (f32[384]{0:T(512)S(1)}, f32[384]{0:T(512)S(1)}, f32[384]{0:T(512)S(1)}, f32[384]{0:T(512)S(1)}, f32[384]{0:T(512)S(1)}, /*index=5*/f32[384]{0:T(5...) fusion(bf16[16,176,384]{2,1,0:T(8,128)(2,1)S(1)} %bitcast.86, bf16[22,182,192]{2,1,0:T(8,128)(2,1)} %collective-permute-done.2, ...), kind=kLoop, calls=%fused_computation.330 | loop fusion | flops 59470464 | bytes 5251584 | tf_op jit(solution)/shard_map/reduce_sum | solution.py:53
  366.8 17.0 %fusion.126 = (f32[384]{0:T(512)S(1)}, f32[384]{0:T(512)S(1)}, f32[384]{0:T(512)S(1)}, f32[384]{0:T(512)S(1)}, f32[384]{0:T(512)S(1)}, /*index=5*/f32[384]{0:T(5...) fusion(bf16[16,176,384]{2,1,0:T(8,128)(2,1)S(1)} %bitcast.87, bf16[22,182,192]{2,1,0:T(8,128)(2,1)} %collective-permute-done.2, ...), kind=kLoop, calls=%fused_computation.331 | loop fusion | flops 59470464 | bytes 5251584 | tf_op jit(solution)/shard_map/reduce_sum | solution.py:53
  383.9 17.8 %fusion.129 = (f32[384]{0:T(512)S(1)}, f32[384]{0:T(512)S(1)}, f32[384]{0:T(512)S(1)}, f32[384]{0:T(512)S(1)}, f32[384]{0:T(512)S(1)}, /*index=5*/f32[384]{0:T(5...) fusion(bf16[16,176,384]{2,1,0:T(8,128)(2,1)S(1)} %bitcast.88, bf16[22,182,192]{2,1,0:T(8,128)(2,1)} %collective-permute-done.2, ...), kind=kLoop, calls=%fused_computation.334 | loop fusion | flops 59470464 | bytes 5251584 | tf_op jit(solution)/shard_map/reduce_sum | solution.py:53
  401.8 17.4 %fusion.128 = (f32[384]{0:T(512)S(1)}, f32[384]{0:T(512)S(1)}, f32[384]{0:T(512)S(1)}, f32[384]{0:T(512)S(1)}, f32[384]{0:T(512)S(1)}, /*index=5*/f32[384]{0:T(5...) fusion(bf16[16,176,384]{2,1,0:T(8,128)(2,1)S(1)} %bitcast.89, bf16[22,182,192]{2,1,0:T(8,128)(2,1)} %collective-permute-done.2, ...), kind=kLoop, calls=%fused_computation.333 | loop fusion | flops 59470464 | bytes 5251584 | tf_op jit(solution)/shard_map/reduce_sum | solution.py:53
  419.2 17.3 %fusion.127 = (f32[384]{0:T(512)S(1)}, f32[384]{0:T(512)S(1)}, f32[384]{0:T(512)S(1)}, f32[384]{0:T(512)S(1)}, f32[384]{0:T(512)S(1)}, /*index=5*/f32[384]{0:T(5...) fusion(bf16[16,176,384]{2,1,0:T(8,128)(2,1)S(1)} %bitcast.90, bf16[22,182,192]{2,1,0:T(8,128)(2,1)} %collective-permute-done.2, ...), kind=kLoop, calls=%fused_computation.332 | loop fusion | flops 59470464 | bytes 5251584 | tf_op jit(solution)/shard_map/reduce_sum | solution.py:53
  439.4 4.7 collective-permute-start.6
  450.8 7.5 %reshape.698 = bf16[16,11,16,2,192]{4,3,2,1,0:T(2,128)(2,1)} reshape(bf16[2816,384]{1,0:T(8,128)(2,1)} %get-tuple-element.184) | data formatting | bytes 4325376 | tf_op jit(solution)/shard_map/reshape | solution.py:151
  462.3 5.8 reshape.699
  468.0 4.2 gather_fusion.1
  476.9 6.8 %all-to-all-start = ((bf16[32,16,3072]{2,1,0:T(8,128)(2,1)}), bf16[32,16,3072]{2,1,0:T(8,128)(2,1)}, u32[]{:S(2)}, u32[]{:S(2)}) async-start(bf16[32,16,3072]{2,1,0:T(8,128)(2,1)} %broadcast_select_fusion.2), calls=%async_computation | async-start | bytes 6291456 | tf_op jit(solution)/shard_map/all_to_all | solution.py:161
  484.0 6.3 maximum_maximum_fusion
  495.3 58.0 %select_convert_fusion = bf16[16,176,384]{2,1,0:T(8,128)(2,1)S(1)} fusion(bf16[16,176,384]{2,1,0:T(8,128)(2,1)} %bitcast.93, bf16[3,176,384]{2,1,0:T(8,128)(2,1)S(1)} %collective-permute-done.7, bf16[3,176,384]{2,1,0:T(8,128)(2,1)} %copy-done.14, bf16[22,179,384]{2,1,0:T(8,128)(2,1)} %get-tuple-element.188, ...), kind=kLoop, calls=%fused_computation.341 | loop fusion | flops 166526976 | bytes 96044720 | tf_op jit(solution)/shard_map/convert_element_type | solution.py:214
  556.1 77.4 %psum.21 = f32[10944]{0:T(1024)S(1)} all-reduce(f32[10944]{0:T(1024)S(1)} %maximum_add_fusion), channel_id=1, replica_groups=mesh['tiles'=16,'chan'=2] {'tiles'}, use_global_device_ids=true, to_apply=%region_63.64 | all-reduce | flops 10944 | bytes 87552 | tf_op jit(solution)/shard_map/psum | solution.py:230
  640.8 19.2 %all-reduce.3.cloned.1.call-done = (f32[384,768]{1,0:T(8,128)}, f32[768,384]{0,1:T(8,128)}) async-done(((f32[384,768]{1,0:T(8,128)}, f32[768,384]{0,1:T(8,128)}), (f32[384,768]{1,0:T(8,128)}, f32[768,384]{0,1:T(8,128)})) %all-reduce.3.cloned.1.call-update) | async-done | bytes 2359312 | tf_op jit(solution)/shard_map/psum | solution.py:197
  (373 shorter events, 100.0 us)
Async XLA Ops:
  9.0 116.6 %collective-permute-start.3 = (f32[10944]{0:T(1024)S(1)}, f32[10944]{0:T(1024)S(1)}, u32[]{:S(2)}, u32[]{:S(2)}) collective-permute-start(f32[10944]{0:T(1024)S(1)} %concatenate.132), channel_id=1, source_target_pairs={{0,1},{1,0},{2,3},{3,2},{4,5},{5,4},{6,7},{7,6},{8,9},{9,8},{10,11... | collective-permute-start | bytes 131336 | tf_op jit(solution)/shard_map/ppermute | solution.py:13
  11.7 119.6 %collective-permute-start.5 = (bf16[768,384]{0,1:T(8,128)(2,1)}, bf16[768,384]{0,1:T(8,128)(2,1)}, u32[]{:S(2)}, u32[]{:S(2)}) collective-permute-start(bf16[768,384]{0,1:T(8,128)(2,1)} %copy.101), channel_id=1, source_target_pairs={{0,1},{1,0},{2,3},{3,2},{4,5},{5,4},{6,7},{7,6},{8,9},{9,8},{10,11... | collective-permute-start | bytes 1769480 | tf_op jit(solution)/shard_map/ppermute | solution.py:13
  11.7 118.4 %collective-permute-start.4 = (bf16[384,768]{1,0:T(8,128)(2,1)}, bf16[384,768]{1,0:T(8,128)(2,1)}, u32[]{:S(2)}, u32[]{:S(2)}) collective-permute-start(bf16[384,768]{1,0:T(8,128)(2,1)} %param.17), channel_id=1, source_target_pairs={{0,1},{1,0},{2,3},{3,2},{4,5},{5,4},{6,7},{7,6},{8,9},{9,8},{10,11... | collective-permute-start | bytes 1769480 | tf_op jit(solution)/shard_map/ppermute | solution.py:13
  21.3 79.0 %collective-permute-start.1 = (bf16[3,352,192]{1,2,0:T(8,128)(2,1)S(1)}, bf16[3,352,192]{1,2,0:T(8,128)(2,1)}, u32[]{:S(2)}, u32[]{:S(2)}) collective-permute-start(bf16[3,352,192]{1,2,0:T(8,128)(2,1)S(1)} %copy.97), channel_id=1, source_target_pairs={{2,0},{4,2},{6,4},{8,6},{10,8},{12,10},{14,12},{16,14},{18,16},{20... | collective-permute-start | bytes 1216520 | tf_op jit(solution)/shard_map/ppermute | solution.py:21
  23.6 78.0 %collective-permute-start = (bf16[3,352,192]{1,2,0:T(8,128)(2,1)}, bf16[3,352,192]{1,2,0:T(8,128)(2,1)}, u32[]{:S(2)}, u32[]{:S(2)}) collective-permute-start(bf16[3,352,192]{1,2,0:T(8,128)(2,1)} %copy.96), channel_id=1, source_target_pairs={{0,2},{2,4},{4,6},{6,8},{8,10},{10,12},{12,14},{14,16},{16,18},{18... | collective-permute-start | bytes 1216520 | tf_op jit(solution)/shard_map/ppermute | solution.py:20
  89.5 166.2 %all-to-all-start.1 = ((bf16[32,16,3072]{2,1,0:T(8,128)(2,1)}), bf16[32,16,3072]{2,1,0:T(8,128)(2,1)}, u32[]{:S(2)}, u32[]{:S(2)}) async-start(bf16[32,16,3072]{2,1,0:T(8,128)(2,1)} %broadcast_select_fusion.1), calls=%async_computation.1 | async-start | bytes 6291456 | tf_op jit(solution)/shard_map/all_to_all | solution.py:98
  123.0 112.0 %copy-start.3 = (bf16[22,182,192]{2,1,0:T(8,128)(2,1)}, bf16[22,182,192]{2,1,0:T(8,128)(2,1)S(1)}, u32[]{:S(2)}) copy-start(bf16[22,182,192]{2,1,0:T(8,128)(2,1)S(1)} %get-tuple-element.186) | copy-start | bytes 4612612
  123.0 12.1 %collective-permute-start.2 = (bf16[22,182,192]{2,1,0:T(8,128)(2,1)}, bf16[22,182,192]{2,1,0:T(8,128)(2,1)}, u32[]{:S(2)}, u32[]{:S(2)}) collective-permute-start(bf16[22,182,192]{2,1,0:T(8,128)(2,1)} %get-tuple-element.185), channel_id=1, source_target_pairs={{0,1},{1,0},{2,3},{3,2},{4,5},{5,4},{6,7},{7,6},{8,9},{9,8},{10,11... | collective-permute-start | bytes 4612616 | tf_op jit(solution)/shard_map/ppermute | solution.py:13
  127.2 107.2 %copy-start.26 = (f32[384]{0:T(512)}, f32[384]{0:T(512)S(1)}, u32[]{:S(2)}) copy-start(f32[384]{0:T(512)S(1)} %get-tuple-element.170) | copy-start | bytes 4612
  127.3 107.2 %copy-start.27 = (f32[384]{0:T(512)}, f32[384]{0:T(512)S(1)}, u32[]{:S(2)}) copy-start(f32[384]{0:T(512)S(1)} %get-tuple-element.171) | copy-start | bytes 4612
  127.3 107.2 %copy-start.28 = (f32[384]{0:T(512)}, f32[384]{0:T(512)S(1)}, u32[]{:S(2)}) copy-start(f32[384]{0:T(512)S(1)} %get-tuple-element.172) | copy-start | bytes 4612
  127.3 107.2 %copy-start.29 = (f32[384]{0:T(512)}, f32[384]{0:T(512)S(1)}, u32[]{:S(2)}) copy-start(f32[384]{0:T(512)S(1)} %get-tuple-element.173) | copy-start | bytes 4612
  127.4 107.1 %copy-start.30 = (f32[384]{0:T(512)}, f32[384]{0:T(512)S(1)}, u32[]{:S(2)}) copy-start(f32[384]{0:T(512)S(1)} %get-tuple-element.161) | copy-start | bytes 4612
  127.4 107.1 %copy-start.31 = (f32[384]{0:T(512)}, f32[384]{0:T(512)S(1)}, u32[]{:S(2)}) copy-start(f32[384]{0:T(512)S(1)} %get-tuple-element.162) | copy-start | bytes 4612
  127.4 107.1 %copy-start.32 = (f32[384]{0:T(512)}, f32[384]{0:T(512)S(1)}, u32[]{:S(2)}) copy-start(f32[384]{0:T(512)S(1)} %get-tuple-element.163) | copy-start | bytes 4612
  127.4 107.1 %copy-start.33 = (f32[384]{0:T(512)}, f32[384]{0:T(512)S(1)}, u32[]{:S(2)}) copy-start(f32[384]{0:T(512)S(1)} %get-tuple-element.164) | copy-start | bytes 4612
  127.4 107.1 %copy-start.34 = (f32[384]{0:T(512)}, f32[384]{0:T(512)S(1)}, u32[]{:S(2)}) copy-start(f32[384]{0:T(512)S(1)} %get-tuple-element.165) | copy-start | bytes 4612
  127.4 107.1 %copy-start.35 = (f32[384]{0:T(512)}, f32[384]{0:T(512)S(1)}, u32[]{:S(2)}) copy-start(f32[384]{0:T(512)S(1)} %get-tuple-element.166) | copy-start | bytes 4612
  127.5 107.1 %copy-start.36 = (f32[384]{0:T(512)}, f32[384]{0:T(512)S(1)}, u32[]{:S(2)}) copy-start(f32[384]{0:T(512)S(1)} %get-tuple-element.167) | copy-start | bytes 4612
  127.5 107.1 %copy-start.37 = (f32[384]{0:T(512)}, f32[384]{0:T(512)S(1)}, u32[]{:S(2)}) copy-start(f32[384]{0:T(512)S(1)} %get-tuple-element.168) | copy-start | bytes 4612
  127.5 107.1 %copy-start.38 = (f32[384]{0:T(512)}, f32[384]{0:T(512)S(1)}, u32[]{:S(2)}) copy-start(f32[384]{0:T(512)S(1)} %get-tuple-element.169) | copy-start | bytes 4612
  131.2 110.3 %copy-start.17 = (bf16[384,1536]{1,0:T(8,128)(2,1)}, bf16[384,1536]{1,0:T(8,128)(2,1)S(1)}, u32[]{:S(2)}) copy-start(bf16[384,1536]{1,0:T(8,128)(2,1)S(1)} %constant_dynamic-update-slice_fusion) | copy-start | bytes 3538948
  340.0 132.2 %copy-start.2 = (bf16[2816,384]{1,0:T(8,128)(2,1)}, bf16[2816,384]{1,0:T(8,128)(2,1)S(1)}, u32[]{:S(2)}) copy-start(bf16[2816,384]{1,0:T(8,128)(2,1)S(1)} %multiply_convert_fusion.1) | copy-start | bytes 6488068
  437.9 117.4 %collective-permute-start.10 = (f32[10944]{0:T(1024)}, f32[10944]{0:T(1024)}, u32[]{:S(2)}, u32[]{:S(2)}) collective-permute-start(f32[10944]{0:T(1024)} %pad_maximum_fusion.9), channel_id=1, source_target_pairs={{0,1},{1,0},{2,3},{3,2},{4,5},{5,4},{6,7},{7,6},{8,9},{9,8},{10,11... | collective-permute-start | bytes 131336 | tf_op jit(solution)/shard_map/ppermute | solution.py:13
  438.1 34.1 %collective-permute-start.7 = (bf16[3,176,384]{2,1,0:T(8,128)(2,1)}, bf16[3,176,384]{2,1,0:T(8,128)(2,1)S(1)}, u32[]{:S(2)}, u32[]{:S(2)}) collective-permute-start(bf16[3,176,384]{2,1,0:T(8,128)(2,1)} %bitcast.109), channel_id=1, source_target_pairs={{2,0},{4,2},{6,4},{8,6},{10,8},{12,10},{14,12},{16,14},{18,16},{20... | collective-permute-start | bytes 1216520 | tf_op jit(solution)/shard_map/ppermute | solution.py:21
  439.4 32.8 %collective-permute-start.6 = (bf16[3,176,384]{2,1,0:T(8,128)(2,1)S(1)}, bf16[3,176,384]{2,1,0:T(8,128)(2,1)S(1)}, u32[]{:S(2)}, u32[]{:S(2)}) collective-permute-start(bf16[3,176,384]{2,1,0:T(8,128)(2,1)S(1)} %bitcast.108), channel_id=1, source_target_pairs={{0,2},{2,4},{4,6},{6,8},{8,10},{10,12},{12,14},{14,16},{16,18},{18... | collective-permute-start | bytes 1216520 | tf_op jit(solution)/shard_map/ppermute | solution.py:20
  447.5 42.8 %collective-permute-start.11 = (f32[384,768]{1,0:T(8,128)}, f32[384,768]{1,0:T(8,128)}, u32[]{:S(2)}, u32[]{:S(2)}) collective-permute-start(f32[384,768]{1,0:T(8,128)} %slice.1161), channel_id=1, source_target_pairs={{0,1},{1,0},{2,3},{3,2},{4,5},{5,4},{6,7},{7,6},{8,9},{9,8},{10,11... | collective-permute-start | bytes 3538952 | tf_op jit(solution)/shard_map/ppermute | solution.py:13
  450.8 42.0 %collective-permute-start.12 = (f32[768,384]{0,1:T(8,128)}, f32[768,384]{0,1:T(8,128)}, u32[]{:S(2)}, u32[]{:S(2)}) collective-permute-start(f32[768,384]{0,1:T(8,128)} %slice.1166), channel_id=1, source_target_pairs={{0,1},{1,0},{2,3},{3,2},{4,5},{5,4},{6,7},{7,6},{8,9},{9,8},{10,11... | collective-permute-start | bytes 3538952 | tf_op jit(solution)/shard_map/ppermute | solution.py:13
  472.3 11.4 %collective-permute-start.8 = (bf16[22,6,384]{2,1,0:T(8,128)(2,1)S(1)}, bf16[22,6,384]{2,1,0:T(8,128)(2,1)S(1)}, u32[]{:S(2)}, u32[]{:S(2)}) collective-permute-start(bf16[22,6,384]{2,1,0:T(8,128)(2,1)S(1)} %fusion.207), channel_id=1, source_target_pairs={{0,1},{1,0},{2,3},{3,2},{4,5},{5,4},{6,7},{7,6},{8,9},{9,8},{10,11... | collective-permute-start | bytes 304136 | tf_op jit(solution)/shard_map/ppermute | solution.py:13
  476.9 185.9 %all-to-all-start = ((bf16[32,16,3072]{2,1,0:T(8,128)(2,1)}), bf16[32,16,3072]{2,1,0:T(8,128)(2,1)}, u32[]{:S(2)}, u32[]{:S(2)}) async-start(bf16[32,16,3072]{2,1,0:T(8,128)(2,1)} %broadcast_select_fusion.2), calls=%async_computation | async-start | bytes 6291456 | tf_op jit(solution)/shard_map/all_to_all | solution.py:161
  483.7 176.3 %all-reduce.3.cloned.1.call-start = ((), (), s32[]{:S(2)}) async-start(), calls=%async_computation.2 | async-start | bytes 4718592 | tf_op jit(solution)/shard_map/psum | solution.py:197
  555.1 80.5 %collective-permute-start.9 = (bf16[16,176,192]{2,1,0:T(8,128)(2,1)}, bf16[16,176,192]{2,1,0:T(8,128)(2,1)S(1)}, u32[]{:S(2)}, u32[]{:S(2)}) collective-permute-start(bf16[16,176,192]{2,1,0:T(8,128)(2,1)} %get-tuple-element.196), channel_id=1, source_target_pairs={{0,1},{1,0},{2,3},{3,2},{4,5},{5,4},{6,7},{7,6},{8,9},{9,8},{10,11... | collective-permute-start | bytes 3244040 | tf_op jit(solution)/shard_map/ppermute | solution.py:13
  (68 other events, 3041.8 us)
Sparse Core Ops, SparseCore 0:
  495.4 164.5 all-reduce.2

commit v2 on v1

--- a/solution.py
+++ b/solution.py
@@ -32,10 +32,28 @@
     return (gelu_value, gelu_slope)
 
 
+def strips(field, count):
+    rows, cols, chans = field.shape
+    return field.reshape(rows, count, cols // count, chans).transpose(0, 2, 1, 3)
+
+
+def unstrip(value):
+    rows, cols, count, chans = value.shape
+    return value.transpose(0, 2, 1, 3).reshape(rows, count * cols, chans)
+
+
+def framed_strips(padded, count, reach):
+    width = padded.shape[1] - reach
+    body = strips(padded[:, :width], count)
+    last = padded[:, width:][:, :, None]
+    tail = jnp.concatenate([body[:, :reach, 1:], last], axis=2)
+    return jnp.concatenate([body, tail], axis=1)
+
+
 def depthwise(padded, kernel):
     span = kernel.shape[0]
     rows, cols = padded.shape[0] - span + 1, padded.shape[1] - span + 1
-    total = jnp.zeros((rows, cols, padded.shape[2]), jnp.float32)
+    total = jnp.zeros((rows, cols) + padded.shape[2:], jnp.float32)
     for down in range(span):
         for east in range(span):
             window = padded[down : down + rows, east : east + cols]
@@ -50,7 +68,7 @@
     for down in range(span):
         for east in range(span):
             window = framed[down : down + rows, east : east + cols].astype(jnp.float32)
-            sums.append(jnp.sum(back_float * window, axis=(0, 1)))
+            sums.append(jnp.sum(back_float * window, axis=(0, 1, 2)))
     return jnp.stack(sums)
 
 
@@ -133,8 +151,9 @@
     kept = lax.dynamic_slice(tall, (0, core * width, 0), shape)
     given = lax.dynamic_slice(tall, (0, (1 - core) * width, 0), shape)
     framed = jnp.concatenate([kept, swapped(given)], axis=2)
-
-    on_land = jnp.repeat(flags, side)[None, :, None] == 0
+    framed = framed_strips(framed, side, 2 * margin)
+
+    on_land = strips(jnp.repeat(flags, side)[None, :, None], side) == 0
     mixed = jnp.where(on_land, 0.0, depthwise(framed, kernel)).reshape(cells, chans)
     cell_mean = jnp.sum(mixed, axis=1) / chans
     variance = jnp.sum(mixed * mixed, axis=1) / chans - cell_mean * cell_mean
@@ -145,10 +164,10 @@
     active, slope = gelu_pair(hidden)
     active = active.astype(jnp.bfloat16)
     branch = jnp.dot(active, w_out, preferred_element_type=jnp.float32) + bias_o
-    residual = framed[margin : margin + side, margin : margin + width]
+    residual = framed[margin : margin + side, margin : margin + half]
     residual = residual.astype(jnp.float32).reshape(cells, chans)
     block = (residual + scale * branch).astype(jnp.bfloat16)
-    block = block.reshape(side, half, side, 2, own).transpose(1, 3, 0, 2, 4)
+    block = unstrip(block.reshape(side, half, side, chans)).reshape(side, half, side, 2, own).transpose(1, 3, 0, 2, 4)
     block = block.reshape(half * 2, side, side * own)
 
     target = jnp.arange(devices, dtype=jnp.int32)
@@ -170,7 +189,7 @@
     pick = pick * cap + (local // devices)[:, None]
     upstream = jnp.take(landed, pick.reshape(-1), axis=0)
     upstream = upstream.reshape(half, 2, side, side, own).transpose(2, 0, 3, 1, 4)
-    upstream = upstream.reshape(side, width, chans).astype(jnp.float32)
+    upstream = strips(upstream.reshape(side, width, chans), side).astype(jnp.float32)
     upstream = jnp.where(on_land, 0.0, upstream).reshape(cells, chans)
     scaled = scale * upstream
     scaled_bf = scaled.astype(jnp.bfloat16)
@@ -194,7 +213,6 @@
     norm_cells = float(devices * listed * side * side) ** 0.5
     grad_w_in = (grad_w_in[:, :group] + swapped(grad_w_in[:, group:])) / norm_cells
     grad_w_out = (grad_w_out[:group] + swapped(grad_w_out[group:])) / norm_cells
-    grad_w_in, grad_w_out = lax.psum((grad_w_in, grad_w_out), "tiles")
 
     back_normed = back_features * gain
     grad_gain = jnp.sum(back_features * normed, axis=0)
@@ -202,16 +220,16 @@
     first = jnp.sum(back_normed, axis=1) / chans
     second = jnp.sum(back_normed * normed, axis=1) / chans
     back_mixed = factor[:, None] * (back_normed - first[:, None] - normed * second[:, None])
-    back = back_mixed.astype(jnp.bfloat16).reshape(side, width, chans)
-
-    back_tall = row_halo(back, margin)
+    back = back_mixed.astype(jnp.bfloat16).reshape(side, half, side, chans)
+
+    back_tall = row_halo(unstrip(back), margin)
     rims = swapped(
         jnp.concatenate([back_tall[:, :margin], back_tall[:, width - margin :]], axis=1)
     )
     rims = jnp.concatenate([rims[..., own:], rims[..., :own]], axis=2)
     back_framed = jnp.concatenate([rims[:, margin:], back_tall, rims[:, :margin]], axis=1)
-    grad_field = depthwise(back_framed, kernel[::-1, ::-1])
-    grad_field = jnp.where(on_land, 0.0, grad_field).astype(jnp.bfloat16)
+    grad_field = depthwise(framed_strips(back_framed, side, 2 * margin), kernel[::-1, ::-1])
+    grad_field = unstrip(jnp.where(on_land, 0.0, grad_field).astype(jnp.bfloat16))
     grad_kept, grad_got = grad_field[..., :own], swapped(grad_field[..., own:])
     grad_cells = jnp.where(
         core == 0,
@@ -227,7 +245,14 @@
     )
     keep = jnp.concatenate([by_channel[:, :own].reshape(-1), grad_bias_in[:group]])
     give = jnp.concatenate([by_channel[:, own:].reshape(-1), grad_bias_in[group:]])
-    summed = lax.psum(keep + swapped(give), "tiles") / norm_cells
+    small = (keep + swapped(give)) / norm_cells
+    lines = -(-small.shape[0] // chans)
+    small = jnp.pad(small, (0, lines * chans - small.shape[0])).reshape(lines, chans)
+    together = jnp.concatenate([grad_w_out, grad_w_in.reshape(group, chans), small], axis=0)
+    together = lax.psum(together, "tiles")
+    grad_w_out = together[:group]
+    grad_w_in = together[group : 2 * group].reshape(chans, group)
+    summed = together[2 * group :].reshape(-1)
     ends_at = span * span * own
     rows = summed[ends_at : ends_at + 4 * own].reshape(4, own)
     return (
@@ -237,7 +262,7 @@
         rows[0],
         rows[1],
         grad_w_in,
-        summed[ends_at + 4 * own :],
+        summed[ends_at + 4 * own : ends_at + 4 * own + group],
         grad_w_out,
         rows[2],
         rows[3],

time: 682 us -> 601 us (0.88)
  other arithmetic: 329 us -> 224 us
  blocking collectives: 127 us -> 49.7 us
  waiting for transfers between devices: 19.2 us -> 94 us
  local copies, waits for them, and re-layouts: 93.9 us -> 125 us
    psum x1 -> x0, blocking collectives: 77.4 us -> none  [on_device(): summed = lax.psum(keep + swapped(give), 'tiles') / norm_cells]
    reduce_sum x6 -> x3, other arithmetic: 95.2 us -> 31.4 us  [kernel_grads(): sums.append(jnp.sum(back_float * window, axis=(0, 1, 2)))]
    reduce_sum x1, other arithmetic: 99.4 us -> 35.9 us  [on_device(): cell_mean = jnp.sum(mixed, axis=1) / chans]
    psum x1, waiting for transfers between devices: 19.2 us -> 58.5 us  [on_device(): together = lax.psum(together, 'tiles')]
    convert_element_type x3, other arithmetic: 66.1 us -> 105 us  [the longest x1 95.1 us: on_device(): jnp.where(on_land, 0.0, grad_field).astype(jnp.bfloat16)]
    ppermute x2, waiting for transfers between devices: 0.01 us -> 27.8 us  [row_halo(): high = lax.ppermute(field[:width], 'tiles', backward)]
    transpose x0 -> x3, local copies, waits for them, and re-layouts: none -> 13.1 us  [the longest x1 5.28 us: on_device(): unstrip(block.reshape(side, half, side, chans))]
    concatenate x1, other arithmetic: 15.4 us -> 4.31 us  [on_device(): jnp.concatenate([tall[:, slots * side - margin:], tall, tall[:, :margin]]...]
  transfers between devices with their start and end apart: 16 -> 16, of which waited for: 1 -> 5; matrix products, arithmetic and copies ran while one was open for 44% -> 47% of each run, Pallas kernels for 0% -> 0%
where the time goes in v2:
time: 601 us; the launch traced here: 595 us
  other arithmetic  224 us (37%)
  local copies, waits for them, and re-layouts  125 us (21%)
  waiting for transfers between devices  94 us (16%)
  matrix products  60.9 us (10%)
  blocking collectives  49.7 us (8%)
  starting transfers between devices  24.6 us (4%)
  between operations  16.9 us (3%)
    convert_element_type x1, other arithmetic, on_device(): jnp.where(on_land, 0.0, grad_field).astype(jnp.bfloat16)  95.1 us
    psum x1, waiting for transfers between devices, on_device(): together = lax.psum(together, 'tiles')  58.5 us
    all_gather x1, blocking collectives, on_device(): masks = lax.all_gather(land_mask[0], 'tiles')  49.7 us
    reduce_sum x1, other arithmetic, on_device(): cell_mean = jnp.sum(mixed, axis=1) / chans  35.9 us
    reduce_sum x3, other arithmetic, kernel_grads(): sums.append(jnp.sum(back_float * window, axis=(0, 1, 2)))  31.4 us
    ppermute x2, waiting for transfers between devices, row_halo(): high = lax.ppermute(field[:width], 'tiles', backward)  27.8 us
    dot_general x1, matrix products, on_device(): jnp.dot(scaled_bf, w_out.T, preferred_element_type=jnp.float32) * slope  19.2 us
    dot_general x1, matrix products, on_device(): jnp.dot(features, w_in, preferred_element_type=jnp.float32) + bias_h  12.8 us
  transfers between devices with their start and end apart: 16, of which 5 were waited for; matrix products, arithmetic and copies ran while one was open for 47% of the time, Pallas kernels for 0%

profile of v2, /device:TPU:0, one launch (start us, length us, event | category | flops | bytes accessed | tf_op | source)
XLA Modules:
  0.0 595.4 jit_solution(14905916077269955366)
XLA Ops:
  12.8 6.0 %reshape_squeeze.3 = bf16[22,16,16,192]{3,2,1,0:T(8,128)(2,1)} reshape(bf16[1,22,1,16,3072]{4,3,2,1,0:T(8,128)(2,1)} %param.11) | data formatting | bytes 4325376 | tf_op jit(solution)/shard_map/reshape;squeeze | solution.py:143
  25.8 5.8 collective-permute-start
  32.0 49.7 %all-gather = s32[16,1,22]{2,1,0:T(1,128)S(1)} all-gather(s32[1,1,22]{2,1,0:T(1,128)S(1)} %bitcast.164), channel_id=1, replica_groups=mesh['tiles'=16,'chan'=2] {'tiles'}, dimensions={0}, use_global_device_ids=true | all-gather | bytes 1496 | tf_op jit(solution)/shard_map/all_gather | solution.py:103
  88.0 3.9 broadcast_select_fusion.1
  96.8 5.0 copy.214
  105.6 4.3 fusion.6
  128.0 35.9 %fusion.163 = (f32[16,11,16]{0,1,2:T(8,128)S(1)}, f32[16,11,16]{0,1,2:T(8,128)S(1)}, f32[16,11,16,384]{3,0,1,2:T(8,128)}) fusion(f32[384]{0:T(512)S(1)} %get-tuple-element.189, bf16[22,17,16,384]{3,0,1,2:T(8,128)(2,1)S(1)} %maximum_maximum_fusion, f32[384]{0:T(512)} %get-tuple-element.142, f32[384]{0:T(512)} %get-tuple-element.143, ...), kind=kLoop, calls=%fused_computation.448 | loop fusion | flops 162195968 | bytes 110395056 | tf_op jit(solution)/shard_map/reduce_sum | solution.py:158
  175.9 12.8 %multiply_convert_fusion = (bf16[2816,1536]{1,0:T(8,128)(2,1)}, f32[2816,1536]{1,0:T(8,128)}) fusion(f32[1536]{0:T(1024)S(1)} %pad_maximum_fusion.14, bf16[2816,384]{1,0:T(8,128)(2,1)S(1)} %add_convert_fusion, bf16[384,1536]{1,0:T(8,128)(2,1)S(1)} %copy-done.18, bf16[192,1536]{1,0:T(8,128)(2,1)S(1)} %copy-done.23, bf16[192,1536]{1,0:T(8,128)(2,1)S(1)} %copy-done.21, ...), kind=kOutput, calls=%fused_computation.62 | convolution fusion | flops 3368091648 | bytes 30480384 | tf_op jit(solution)/shard_map/dot_general | solution.py:163
  188.7 4.0 gather_fusion.4
  192.8 6.0 %gather.32 = bf16[11,2,16,16,192]{4,3,2,1,0:T(8,128)(2,1)} reshape(bf16[22,16,3072]{2,1,0:T(8,128)(2,1)} %gather_fusion.4) | data formatting | bytes 4325376 | tf_op jit(solution)/shard_map/jit(_take)/gather | solution.py:190
  198.7 7.5 %convert_bitcast_fusion = f32[16,11,16,2,192]{4,3,0,2,1:T(2,128)} fusion(pred[11,2]{1,0:T(8,128)(4,1)S(1)} %copy.233, bf16[11,2,16,16,192]{4,3,2,1,0:T(8,128)(2,1)} %gather.32), kind=kLoop, calls=%fused_computation.63 | loop fusion | flops 2162688 | bytes 6488086 | tf_op jit(solution)/shard_map/convert_element_type | solution.py:192
  206.3 8.0 %reshape.815 = f32[16,16,11,384]{3,0,2,1:T(8,128)} reshape(f32[16,11,16,2,192]{4,3,0,2,1:T(2,128)} %convert_bitcast_fusion) | data formatting | bytes 8650752 | tf_op jit(solution)/shard_map/convert_element_type | solution.py:192
  218.8 10.9 %fusion.106 = (f32[384]{0:T(512)S(1)}, bf16[2816,384]{1,0:T(8,128)(2,1)}, bf16[2816,384]{1,0:T(8,128)(2,1)}) fusion(f32[16,11,16,384]{3,2,1,0:T(8,128)S(1)} %copy.237, f32[384]{0:T(512)S(1)} %get-tuple-element.243, f32[16,11,16,384]{3,2,1,0:T(8,128)S(1)} %bitcast.153, f32[384]{0:T(512)S(1)} %get-tuple-element.244, ...), kind=kOutput, calls=%fused_computation.221 | convolution fusion | flops 3335847424 | bytes 23990784 | tf_op jit(solution)/shard_map/dot_general | solution.py:166
  229.7 6.8 %fusion.179 = f32[1536,384]{0,1:T(8,128)} fusion(bf16[2816,1536]{1,0:T(8,128)(2,1)S(1)} %bitcast.167, bf16[2816,384]{1,0:T(8,128)(2,1)} %get-tuple-element.202), kind=kOutput, calls=%fused_computation.463 | convolution fusion | flops 3321888768 | bytes 13172736 | tf_op jit(solution)/shard_map/dot_general | solution.py:198
  236.6 19.2 %fusion.178 = (f32[1536]{0:T(1024)S(1)}, bf16[2816,1536]{1,0:T(8,128)(2,1)S(1)}) fusion(f32[2816,1536]{1,0:T(8,128)} %get-tuple-element.239, f32[1536]{0:T(1024)S(1)} %pad_maximum_fusion.14, bf16[2816,384]{1,0:T(8,128)(2,1)} %get-tuple-element.202, bf16[768,384]{0,1:T(8,128)(2,1)} %collective-permute-done.5, bf16[768,384]{0,1:T(8,128)(2,1)} %copy.228, ...), kind=kOutput, calls=%fused_computation.462 | convolution fusion | flops 3418028544 | bytes 30486528 | tf_op jit(solution)/shard_map/dot_general | solution.py:199
  255.8 4.9 fusion.109
  260.8 6.2 %multiply_reduce_fusion.1 = (f32[384]{0:T(512)}, f32[2816]{0:T(1024)S(1)}, f32[2816]{0:T(1024)S(1)}, f32[384]{0:T(512)S(1)}, f32[2816,384]{1,0:T(8,128)S(1)}) fusion(f32[16,11,16,384]{3,2,1,0:T(8,128)S(1)} %bitcast.146, f32[2816]{0:T(1024)S(1)} %add_rsqrt_fusion, f32[2816]{0:T(1024)S(1)} %div.87, f32[384]{0:T(512)S(1)} %get-tuple-element.245, ...), kind=kOutput, calls=%fused_computation.228 | convolution fusion | flops 3334563328 | bytes 19710464 | tf_op jit(solution)/shard_map/dot_general | solution.py:203
  270.4 6.9 %fusion.98 = (f32[384]{0:T(512)S(1)}, f32[384]{0:T(512)S(1)}, f32[384]{0:T(512)S(1)}, f32[384]{0:T(512)S(1)}, f32[384]{0:T(512)S(1)}, /*index=5*/f32[384]{0:T(51...) fusion(bf16[22,11,16,384]{3,0,1,2:T(8,128)(2,1)S(1)} %bitcast.1, ...), kind=kLoop, calls=%fused_computation.211 | loop fusion | flops 43248768 | bytes 30297600 | tf_op jit(solution)/shard_map/reduce_sum | solution.py:71
  277.4 12.1 %fusion.104 = (f32[384]{0:T(512)S(1)}, f32[384]{0:T(512)S(1)}, f32[384]{0:T(512)S(1)}, f32[384]{0:T(512)S(1)}, f32[384]{0:T(512)S(1)}, /*index=5*/f32[384]{0:T(5...) fusion(bf16[22,17,16,384]{3,0,1,2:T(8,128)(2,1)S(1)} %bitcast.1, ...), kind=kLoop, calls=%fused_computation.217 | loop fusion | flops 59467008 | bytes 41118720 | tf_op jit(solution)/shard_map/reduce_sum | solution.py:71
  289.5 12.3 %fusion.85 = (f32[384]{0:T(512)S(1)}, f32[384]{0:T(512)S(1)}, f32[384]{0:T(512)S(1)}, f32[384]{0:T(512)S(1)}, f32[384]{0:T(512)S(1)}, /*index=5*/f32[384]{0:T(51...) fusion(bf16[22,17,16,384]{3,0,1,2:T(8,128)(2,1)S(1)} %bitcast.1, ...), kind=kLoop, calls=%fused_computation.198 | loop fusion | flops 59467008 | bytes 41118720 | tf_op jit(solution)/shard_map/reduce_sum | solution.py:71
  306.7 7.5 %reshape_reshape.4 = bf16[16,11,16,2,192]{4,3,0,2,1:T(2,128)(2,1)} reshape(bf16[16,16,11,384]{3,0,2,1:T(8,128)(2,1)} %bitcast.151) | data formatting | bytes 4325376 | tf_op jit(solution)/shard_map/reshape;reshape | solution.py:170
  314.1 5.3 copy.230
  319.4 5.8 reshape.801
  325.2 4.2 gather_fusion.1
  329.4 4.0 broadcast_select_fusion.2
  333.4 6.1 %all-to-all-start = ((bf16[32,16,3072]{2,1,0:T(8,128)(2,1)}), bf16[32,16,3072]{2,1,0:T(8,128)(2,1)}, u32[]{:S(2)}, u32[]{:S(2)}) async-start(bf16[32,16,3072]{2,1,0:T(8,128)(2,1)} %broadcast_select_fusion.2), calls=%async_computation | async-start | bytes 6291456 | tf_op jit(solution)/shard_map/all_to_all | solution.py:180
  341.5 4.6 collective-permute-start.6
  351.0 27.8 %collective-permute-done.7 = bf16[3,176,384]{2,1,0:T(8,128)(2,1)S(1)} collective-permute-done((bf16[3,176,384]{2,1,0:T(8,128)(2,1)S(1)}, bf16[3,176,384]{2,1,0:T(8,128)(2,1)S(1)}, u32[]{:S(2)}, u32[]{:S(2)}) %collective-permute-start.7) | collective-permute-done | bytes 405536 | tf_op jit(solution)/shard_map/ppermute | solution.py:21
  386.5 5.4 pad_maximum_fusion.4
  404.1 95.1 %select_convert_fusion = bf16[16,11,16,384]{3,0,1,2:T(8,128)(2,1)S(1)} fusion(bf16[22,17,16,384]{3,0,1,2:T(8,128)(2,1)} %maximum_maximum_fusion.1, bf16[22,11,16,384]{3,0,1,2:T(8,128)(2,1)} %bitcast.136, f32[384]{0:T(512)S(1)} %copy-done.34, f32[384]{0:T(512)} %get-tuple-element.142, f32[384]{0:T(512)} %get-tuple-element.143, f32[384]{0:T(512)} %get-tuple-element.144, ...), kind=kLoop, calls=%fused_computation.229 | loop fusion | flops 160038912 | bytes 108209840 | tf_op jit(solution)/shard_map/convert_element_type | solution.py:232
  509.8 5.8 reshape.807
  515.6 58.5 %all-reduce.3.cloned.1.call-done = f32[1565,384]{0,1:T(8,128)} async-done(((f32[1565,384]{0,1:T(8,128)}), f32[1565,384]{0,1:T(8,128)}) %all-reduce.3.cloned.1.call-update) | async-done | bytes 2403856 | tf_op jit(solution)/shard_map/psum | solution.py:252
  (466 shorter events, 120.2 us)
Async XLA Ops:
  7.2 78.4 %copy-start = (bf16[14,1,16,3072]{3,2,1,0:T(8,128)(2,1)S(1)}, bf16[14,1,16,3072]{3,2,1,0:T(8,128)(2,1)}, u32[]{:S(2)}) copy-start(bf16[14,1,16,3072]{3,2,1,0:T(8,128)(2,1)} %param.13) | copy-start | bytes 4128772
  9.0 104.9 %collective-permute-start.3 = (f32[10944]{0:T(1024)S(1)}, f32[10944]{0:T(1024)S(1)}, u32[]{:S(2)}, u32[]{:S(2)}) collective-permute-start(f32[10944]{0:T(1024)S(1)} %concatenate.99), channel_id=1, source_target_pairs={{0,1},{1,0},{2,3},{3,2},{4,5},{5,4},{6,7},{7,6},{8,9},{9,8},{10,11... | collective-permute-start | bytes 131336 | tf_op jit(solution)/shard_map/ppermute | solution.py:13
  11.6 106.0 %collective-permute-start.5 = (bf16[768,384]{0,1:T(8,128)(2,1)}, bf16[768,384]{0,1:T(8,128)(2,1)}, u32[]{:S(2)}, u32[]{:S(2)}) collective-permute-start(bf16[768,384]{0,1:T(8,128)(2,1)} %copy.228), channel_id=1, source_target_pairs={{0,1},{1,0},{2,3},{3,2},{4,5},{5,4},{6,7},{7,6},{8,9},{9,8},{10,11... | collective-permute-start | bytes 1769480 | tf_op jit(solution)/shard_map/ppermute | solution.py:13
  11.7 104.8 %collective-permute-start.4 = (bf16[384,768]{1,0:T(8,128)(2,1)}, bf16[384,768]{1,0:T(8,128)(2,1)}, u32[]{:S(2)}, u32[]{:S(2)}) collective-permute-start(bf16[384,768]{1,0:T(8,128)(2,1)} %param.17), channel_id=1, source_target_pairs={{0,1},{1,0},{2,3},{3,2},{4,5},{5,4},{6,7},{7,6},{8,9},{9,8},{10,11... | collective-permute-start | bytes 1769480 | tf_op jit(solution)/shard_map/ppermute | solution.py:13
  23.5 78.8 %collective-permute-start.1 = (bf16[3,352,192]{1,2,0:T(8,128)(2,1)}, bf16[3,352,192]{1,2,0:T(8,128)(2,1)}, u32[]{:S(2)}, u32[]{:S(2)}) collective-permute-start(bf16[3,352,192]{1,2,0:T(8,128)(2,1)} %copy.215), channel_id=1, source_target_pairs={{2,0},{4,2},{6,4},{8,6},{10,8},{12,10},{14,12},{16,14},{18,16},{20... | collective-permute-start | bytes 1216520 | tf_op jit(solution)/shard_map/ppermute | solution.py:21
  25.8 78.2 %collective-permute-start = (bf16[3,352,192]{1,2,0:T(8,128)(2,1)}, bf16[3,352,192]{1,2,0:T(8,128)(2,1)}, u32[]{:S(2)}, u32[]{:S(2)}) collective-permute-start(bf16[3,352,192]{1,2,0:T(8,128)(2,1)} %copy.213), channel_id=1, source_target_pairs={{0,2},{2,4},{4,6},{6,8},{8,10},{10,12},{12,14},{14,16},{16,18},{18... | collective-permute-start | bytes 1216520 | tf_op jit(solution)/shard_map/ppermute | solution.py:20
  91.9 96.9 %all-to-all-start.1 = ((bf16[32,16,3072]{2,1,0:T(8,128)(2,1)}), bf16[32,16,3072]{2,1,0:T(8,128)(2,1)}, u32[]{:S(2)}, u32[]{:S(2)}) async-start(bf16[32,16,3072]{2,1,0:T(8,128)(2,1)} %broadcast_select_fusion.1), calls=%async_computation.1 | async-start | bytes 6291456 | tf_op jit(solution)/shard_map/all_to_all | solution.py:116
  113.4 8.2 %collective-permute-start.2 = (bf16[22,182,192]{2,1,0:T(8,128)(2,1)}, bf16[22,182,192]{2,1,0:T(8,128)(2,1)}, u32[]{:S(2)}, u32[]{:S(2)}) collective-permute-start(bf16[22,182,192]{2,1,0:T(8,128)(2,1)} %copy.218), channel_id=1, source_target_pairs={{0,1},{1,0},{2,3},{3,2},{4,5},{5,4},{6,7},{7,6},{8,9},{9,8},{10,11... | collective-permute-start | bytes 4612616 | tf_op jit(solution)/shard_map/ppermute | solution.py:13
  114.2 13.4 %copy-start.27 = (f32[384]{0:T(512)}, f32[384]{0:T(512)S(1)}, u32[]{:S(2)}) copy-start(f32[384]{0:T(512)S(1)} %get-tuple-element.186) | copy-start | bytes 4612
  114.2 13.4 %copy-start.29 = (f32[384]{0:T(512)}, f32[384]{0:T(512)S(1)}, u32[]{:S(2)}) copy-start(f32[384]{0:T(512)S(1)} %get-tuple-element.187) | copy-start | bytes 4612
  114.2 13.4 %copy-start.31 = (f32[384]{0:T(512)}, f32[384]{0:T(512)S(1)}, u32[]{:S(2)}) copy-start(f32[384]{0:T(512)S(1)} %get-tuple-element.188) | copy-start | bytes 4612
  114.2 13.4 %copy-start.33 = (f32[384]{0:T(512)}, f32[384]{0:T(512)S(1)}, u32[]{:S(2)}) copy-start(f32[384]{0:T(512)S(1)} %get-tuple-element.189) | copy-start | bytes 4612
  114.4 13.3 %copy-start.37 = (f32[384]{0:T(512)}, f32[384]{0:T(512)S(1)}, u32[]{:S(2)}) copy-start(f32[384]{0:T(512)S(1)} %get-tuple-element.178) | copy-start | bytes 4612
  114.4 13.3 %copy-start.39 = (f32[384]{0:T(512)}, f32[384]{0:T(512)S(1)}, u32[]{:S(2)}) copy-start(f32[384]{0:T(512)S(1)} %get-tuple-element.179) | copy-start | bytes 4612
  114.4 13.3 %copy-start.41 = (f32[384]{0:T(512)}, f32[384]{0:T(512)S(1)}, u32[]{:S(2)}) copy-start(f32[384]{0:T(512)S(1)} %get-tuple-element.180) | copy-start | bytes 4612
  114.4 13.3 %copy-start.43 = (f32[384]{0:T(512)}, f32[384]{0:T(512)S(1)}, u32[]{:S(2)}) copy-start(f32[384]{0:T(512)S(1)} %get-tuple-element.181) | copy-start | bytes 4612
  114.4 13.3 %copy-start.45 = (f32[384]{0:T(512)}, f32[384]{0:T(512)S(1)}, u32[]{:S(2)}) copy-start(f32[384]{0:T(512)S(1)} %get-tuple-element.182) | copy-start | bytes 4612
  114.4 13.3 %copy-start.47 = (f32[384]{0:T(512)}, f32[384]{0:T(512)S(1)}, u32[]{:S(2)}) copy-start(f32[384]{0:T(512)S(1)} %get-tuple-element.183) | copy-start | bytes 4612
  114.4 13.3 %copy-start.49 = (f32[384]{0:T(512)}, f32[384]{0:T(512)S(1)}, u32[]{:S(2)}) copy-start(f32[384]{0:T(512)S(1)} %get-tuple-element.184) | copy-start | bytes 4612
  114.5 13.3 %copy-start.51 = (f32[384]{0:T(512)}, f32[384]{0:T(512)S(1)}, u32[]{:S(2)}) copy-start(f32[384]{0:T(512)S(1)} %get-tuple-element.185) | copy-start | bytes 4612
  127.6 36.3 %copy-start.2 = (bf16[22,17,16,384]{3,0,1,2:T(8,128)(2,1)}, bf16[22,17,16,384]{3,0,1,2:T(8,128)(2,1)S(1)}, u32[]{:S(2)}) copy-start(bf16[22,17,16,384]{3,0,1,2:T(8,128)(2,1)S(1)} %maximum_maximum_fusion) | copy-start | bytes 13787140
  229.7 31.1 %slice-start.2 = ((s8[4325376]{0:T(1024)(128)(4,1)}), s8[4194304]{0:T(1024)(128)(4,1)S(1)}, s32[]{:S(2)}) async-start(s8[4325376]{0:T(1024)(128)(4,1)} %bitcast.145), calls=%async_computation.5 | async-start | bytes 8388608
  236.5 24.2 %slice-start.3 = ((s8[4325376]{0:T(1024)(128)(4,1)}), s8[131072]{0:T(1024)(128)(4,1)S(1)}, s32[]{:S(2)}) async-start(s8[4325376]{0:T(1024)(128)(4,1)} %bitcast.145), calls=%async_computation.6 | async-start | bytes 262144
  306.4 77.3 %collective-permute-start.12 = (f32[10944]{0:T(1024)S(1)}, f32[10944]{0:T(1024)S(1)}, u32[]{:S(2)}, u32[]{:S(2)}) collective-permute-start(f32[10944]{0:T(1024)S(1)} %pad_maximum_fusion.13), channel_id=1, source_target_pairs={{0,1},{1,0},{2,3},{3,2},{4,5},{5,4},{6,7},{7,6},{8,9},{9,8},{10,11... | collective-permute-start | bytes 131336 | tf_op jit(solution)/shard_map/ppermute | solution.py:13
  333.4 251.0 %all-to-all-start = ((bf16[32,16,3072]{2,1,0:T(8,128)(2,1)}), bf16[32,16,3072]{2,1,0:T(8,128)(2,1)}, u32[]{:S(2)}, u32[]{:S(2)}) async-start(bf16[32,16,3072]{2,1,0:T(8,128)(2,1)} %broadcast_select_fusion.2), calls=%async_computation | async-start | bytes 6291456 | tf_op jit(solution)/shard_map/all_to_all | solution.py:180
  339.5 234.6 %all-reduce.3.cloned.1.call-start = ((), (), s32[]{:S(2)}) async-start(), calls=%async_computation.2 | async-start | bytes 5111808 | tf_op jit(solution)/shard_map/psum | solution.py:252
  340.1 38.7 %collective-permute-start.7 = (bf16[3,176,384]{2,1,0:T(8,128)(2,1)S(1)}, bf16[3,176,384]{2,1,0:T(8,128)(2,1)S(1)}, u32[]{:S(2)}, u32[]{:S(2)}) collective-permute-start(bf16[3,176,384]{2,1,0:T(8,128)(2,1)S(1)} %copy.255), channel_id=1, source_target_pairs={{2,0},{4,2},{6,4},{8,6},{10,8},{12,10},{14,12},{16,14},{18,16},{20... | collective-permute-start | bytes 1216520 | tf_op jit(solution)/shard_map/ppermute | solution.py:21
  341.5 41.2 %collective-permute-start.6 = (bf16[3,176,384]{2,1,0:T(8,128)(2,1)S(1)}, bf16[3,176,384]{2,1,0:T(8,128)(2,1)S(1)}, u32[]{:S(2)}, u32[]{:S(2)}) collective-permute-start(bf16[3,176,384]{2,1,0:T(8,128)(2,1)S(1)} %copy.254), channel_id=1, source_target_pairs={{0,2},{2,4},{4,6},{6,8},{8,10},{10,12},{12,14},{14,16},{16,18},{18... | collective-permute-start | bytes 1216520 | tf_op jit(solution)/shard_map/ppermute | solution.py:20
  347.8 47.8 %collective-permute-start.11 = (f32[384,768]{1,0:T(8,128)}, f32[384,768]{1,0:T(8,128)}, u32[]{:S(2)}, u32[]{:S(2)}) collective-permute-start(f32[384,768]{1,0:T(8,128)} %slice.1108), channel_id=1, source_target_pairs={{0,1},{1,0},{2,3},{3,2},{4,5},{5,4},{6,7},{7,6},{8,9},{9,8},{10,11... | collective-permute-start | bytes 3538952 | tf_op jit(solution)/shard_map/ppermute | solution.py:13
  351.0 48.9 %collective-permute-start.10 = (f32[768,384]{0,1:T(8,128)}, f32[768,384]{0,1:T(8,128)}, u32[]{:S(2)}, u32[]{:S(2)}) collective-permute-start(f32[768,384]{0,1:T(8,128)} %slice.1104), channel_id=1, source_target_pairs={{0,1},{1,0},{2,3},{3,2},{4,5},{5,4},{6,7},{7,6},{8,9},{9,8},{10,11... | collective-permute-start | bytes 3538952 | tf_op jit(solution)/shard_map/ppermute | solution.py:13
  383.7 1.7 collective-permute-start.8
  501.0 3.6 collective-permute-start.9
  (102 other events, 579.8 us)
Sparse Core Ops, SparseCore 0:
  403.9 170.1 all-reduce.2

commit v3 on v2

--- a/solution.py
+++ b/solution.py
@@ -228,8 +228,9 @@
     )
     rims = jnp.concatenate([rims[..., own:], rims[..., :own]], axis=2)
     back_framed = jnp.concatenate([rims[:, margin:], back_tall, rims[:, :margin]], axis=1)
-    grad_field = depthwise(framed_strips(back_framed, side, 2 * margin), kernel[::-1, ::-1])
-    grad_field = unstrip(jnp.where(on_land, 0.0, grad_field).astype(jnp.bfloat16))
+    grad_field = depthwise(back_framed, kernel[::-1, ::-1])
+    land_cols = jnp.repeat(flags, side)[None, :, None] == 0
+    grad_field = jnp.where(land_cols, 0.0, grad_field).astype(jnp.bfloat16)
     grad_kept, grad_got = grad_field[..., :own], swapped(grad_field[..., own:])
     grad_cells = jnp.where(
         core == 0,

time: 601 us -> 629 us (1.047)
  waiting for transfers between devices: 94 us -> 129 us
  other arithmetic: 224 us -> 215 us
    psum x1, waiting for transfers between devices: 58.5 us -> 94.6 us  [on_device(): together = lax.psum(together, 'tiles')]
    convert_element_type x1, other arithmetic: 95.1 us -> 63.9 us  [on_device(): grad_field = jnp.where(land_cols, 0.0, grad_field).astype(jnp.bfloat16)]
    concatenate x1, other arithmetic: 4.31 us -> 16.5 us  [on_device(): jnp.concatenate([tall[:, slots * side - margin:], tall, tall[:, :margin]]...]
    concatenate x1, other arithmetic: 5.44 us -> 12.4 us  [on_device(): jnp.concatenate([rims[:, margin:], back_tall, rims[:, :margin]], axis=1)]
  transfers between devices with their start and end apart: 16 -> 16, of which waited for: 5 -> 5; matrix products, arithmetic and copies ran while one was open for 47% -> 44% of each run, Pallas kernels for 0% -> 0%
where the time goes in v3:
time: 629 us; the launch traced here: 624 us
  other arithmetic  215 us (34%)
  waiting for transfers between devices  129 us (21%)
  local copies, waits for them, and re-layouts  127 us (20%)
  matrix products  61.6 us (10%)
  blocking collectives  49.7 us (8%)
  starting transfers between devices  24.6 us (4%)
  between operations  16.4 us (3%)
    psum x1, waiting for transfers between devices, on_device(): together = lax.psum(together, 'tiles')  94.6 us
    convert_element_type x1, other arithmetic, on_device(): grad_field = jnp.where(land_cols, 0.0, grad_field).astype(jnp.bfloat16)  63.9 us
    all_gather x1, blocking collectives, on_device(): masks = lax.all_gather(land_mask[0], 'tiles')  49.7 us
    reduce_sum x1, other arithmetic, on_device(): cell_mean = jnp.sum(mixed, axis=1) / chans  35.9 us
    reduce_sum x3, other arithmetic, kernel_grads(): sums.append(jnp.sum(back_float * window, axis=(0, 1, 2)))  31.4 us
    ppermute x2, waiting for transfers between devices, row_halo(): high = lax.ppermute(field[:width], 'tiles', backward)  28.3 us
    dot_general x1, matrix products, on_device(): jnp.dot(scaled_bf, w_out.T, preferred_element_type=jnp.float32) * slope  18.7 us
    concatenate x1, other arithmetic, on_device(): jnp.concatenate([tall[:, slots * side - margin:], tall, tall[:, :margin]]...  16.5 us
  transfers between devices with their start and end apart: 16, of which 5 were waited for; matrix products, arithmetic and copies ran while one was open for 44% of the time, Pallas kernels for 0%

profile of v3, /device:TPU:0, one launch (start us, length us, event | category | flops | bytes accessed | tf_op | source)
XLA Modules:
  0.0 624.0 jit_solution(14243579502459703909)
XLA Ops:
  13.4 6.0 reshape_squeeze.3
  26.4 5.8 collective-permute-start
  32.6 49.7 %all-gather = s32[16,1,22]{2,1,0:T(1,128)S(1)} all-gather(s32[1,1,22]{2,1,0:T(1,128)S(1)} %bitcast.150), channel_id=1, replica_groups=mesh['tiles'=16,'chan'=2] {'tiles'}, dimensions={0}, use_global_device_ids=true | all-gather | bytes 1496 | tf_op jit(solution)/shard_map/all_gather | solution.py:103
  89.2 4.0 broadcast_select_fusion.1
  107.8 16.5 %fusion.6 = bf16[22,358,192]{2,0,1:T(8,128)(2,1)S(1)} fusion(bf16[3,352,192]{2,0,1:T(4,128)(2,1)} %copy.216, bf16[16,352,192]{2,0,1:T(8,128)(2,1)S(1)} %bitcast.135, bf16[3,352,192]{2,0,1:T(4,128)(2,1)} %copy.215), kind=kLoop, calls=%fused_computation.115 | loop fusion | flops 27219456 | bytes 5998080 | tf_op jit(solution)/shard_map/concatenate | solution.py:147
  148.2 35.9 %fusion.166 = (f32[16,11,16]{0,1,2:T(8,128)S(1)}, f32[16,11,16]{0,1,2:T(8,128)S(1)}, f32[16,11,16,384]{3,0,1,2:T(8,128)}) fusion(f32[384]{0:T(512)S(1)} %get-tuple-element.189, bf16[22,17,16,384]{3,0,1,2:T(8,128)(2,1)S(1)} %maximum_maximum_fusion, f32[384]{0:T(512)} %get-tuple-element.142, f32[384]{0:T(512)} %get-tuple-element.143, ...), kind=kLoop, calls=%fused_computation.456 | loop fusion | flops 162195968 | bytes 110395056 | tf_op jit(solution)/shard_map/reduce_sum | solution.py:158
  199.0 12.8 %multiply_convert_fusion = (bf16[2816,1536]{1,0:T(8,128)(2,1)}, f32[2816,1536]{1,0:T(8,128)}) fusion(f32[1536]{0:T(1024)S(1)} %copy-done.82, bf16[2816,384]{1,0:T(8,128)(2,1)S(1)} %add_convert_fusion, bf16[384,1536]{1,0:T(8,128)(2,1)S(1)} %copy-done.22, bf16[192,1536]{1,0:T(8,128)(2,1)S(1)} %copy-done.27, bf16[192,1536]{1,0:T(8,128)(2,1)S(1)} %copy-done.25, ...), kind=kOutput, calls=%fused_computation.62 | convolution fusion | flops 3368091648 | bytes 30480384 | tf_op jit(solution)/shard_map/dot_general | solution.py:163
  211.8 4.1 gather_fusion.4
  215.9 6.1 gather.32
  222.1 7.6 %convert_bitcast_fusion = f32[16,11,16,2,192]{4,3,0,2,1:T(2,128)} fusion(pred[11,2]{1,0:T(8,128)(4,1)S(1)} %copy.232, bf16[11,2,16,16,192]{4,3,2,1,0:T(8,128)(2,1)} %gather.32), kind=kLoop, calls=%fused_computation.63 | loop fusion | flops 2162688 | bytes 6488086 | tf_op jit(solution)/shard_map/convert_element_type | solution.py:192
  229.6 7.9 %reshape.769 = f32[16,16,11,384]{3,0,2,1:T(8,128)} reshape(f32[16,11,16,2,192]{4,3,0,2,1:T(2,128)} %convert_bitcast_fusion) | data formatting | bytes 8650752 | tf_op jit(solution)/shard_map/convert_element_type | solution.py:192
  242.0 8.9 %fusion.106 = (f32[384]{0:T(512)S(1)}, bf16[2816,384]{1,0:T(8,128)(2,1)S(1)}, bf16[2816,384]{1,0:T(8,128)(2,1)S(1)}) fusion(f32[16,11,16,384]{3,2,1,0:T(8,128)S(1)} %copy.236, f32[384]{0:T(512)S(1)} %get-tuple-element.245, f32[16,11,16,384]{3,2,1,0:T(8,128)S(1)} %bitcast.140, f32[384]{0:T(512)S(1)} %copy-done.87, ...), kind=kOutput, calls=%fused_computation.220 | convolution fusion | flops 3335847424 | bytes 23990784 | tf_op jit(solution)/shard_map/dot_general | solution.py:166
  250.9 8.6 %fusion.181 = f32[1536,384]{0,1:T(8,128)} fusion(bf16[2816,1536]{1,0:T(8,128)(2,1)} %get-tuple-element.240, bf16[2816,384]{1,0:T(8,128)(2,1)S(1)} %get-tuple-element.202), kind=kOutput, calls=%fused_computation.470 | convolution fusion | flops 3321888768 | bytes 13172736 | tf_op jit(solution)/shard_map/dot_general | solution.py:198
  259.5 18.7 %fusion.180 = (f32[1536]{0:T(1024)S(1)}, bf16[2816,1536]{1,0:T(8,128)(2,1)S(1)}) fusion(f32[2816,1536]{1,0:T(8,128)} %get-tuple-element.241, f32[1536]{0:T(1024)S(1)} %copy-done.82, bf16[2816,384]{1,0:T(8,128)(2,1)S(1)} %get-tuple-element.202, bf16[768,384]{0,1:T(8,128)(2,1)} %collective-permute-done.5, bf16[768,384]{0,1:T(8,128)(2,1)} %copy.227, ...), kind=kOutput, calls=%fused_computation.469 | convolution fusion | flops 3418028544 | bytes 30486528 | tf_op jit(solution)/shard_map/dot_general | solution.py:199
  278.3 5.1 fusion.109
  283.4 7.5 %multiply_reduce_fusion.1 = (f32[384]{0:T(512)S(1)}, f32[2816]{0:T(1024)S(1)}, f32[2816]{0:T(1024)S(1)}, f32[384]{0:T(512)S(1)}, f32[2816,384]{1,0:T(8,128)}) fusion(f32[16,11,16,384]{3,2,1,0:T(8,128)S(1)} %bitcast.134, f32[2816]{0:T(1024)S(1)} %add_rsqrt_fusion, f32[2816]{0:T(1024)S(1)} %div.87, f32[384]{0:T(512)S(1)} %get-tuple-element.247, ...), kind=kOutput, calls=%fused_computation.227 | convolution fusion | flops 3334563328 | bytes 19710464 | tf_op jit(solution)/shard_map/dot_general | solution.py:203
  290.9 4.5 multiply_convert_fusion.1
  295.4 7.0 %fusion.98 = (f32[384]{0:T(512)S(1)}, f32[384]{0:T(512)S(1)}, f32[384]{0:T(512)S(1)}, f32[384]{0:T(512)S(1)}, f32[384]{0:T(512)S(1)}, /*index=5*/f32[384]{0:T(51...) fusion(bf16[22,11,16,384]{3,0,1,2:T(8,128)(2,1)S(1)} %bitcast.1, ...), kind=kLoop, calls=%fused_computation.210 | loop fusion | flops 43248768 | bytes 30297600 | tf_op jit(solution)/shard_map/reduce_sum | solution.py:71
  302.4 12.1 %fusion.85 = (f32[384]{0:T(512)S(1)}, f32[384]{0:T(512)S(1)}, f32[384]{0:T(512)S(1)}, f32[384]{0:T(512)S(1)}, f32[384]{0:T(512)S(1)}, /*index=5*/f32[384]{0:T(51...) fusion(bf16[22,17,16,384]{3,0,1,2:T(8,128)(2,1)S(1)} %bitcast.1, ...), kind=kLoop, calls=%fused_computation.197 | loop fusion | flops 59467008 | bytes 41118720 | tf_op jit(solution)/shard_map/reduce_sum | solution.py:71
  314.5 12.3 %fusion.104 = (f32[384]{0:T(512)S(1)}, f32[384]{0:T(512)S(1)}, f32[384]{0:T(512)S(1)}, f32[384]{0:T(512)S(1)}, f32[384]{0:T(512)S(1)}, /*index=5*/f32[384]{0:T(5...) fusion(bf16[22,17,16,384]{3,0,1,2:T(8,128)(2,1)S(1)} %bitcast.1, ...), kind=kLoop, calls=%fused_computation.216 | loop fusion | flops 59467008 | bytes 41118720 | tf_op jit(solution)/shard_map/reduce_sum | solution.py:71
  330.8 7.5 %reshape_reshape.4 = bf16[16,11,16,2,192]{4,3,0,2,1:T(2,128)(2,1)} reshape(bf16[16,16,11,384]{3,0,2,1:T(8,128)(2,1)} %bitcast.138) | data formatting | bytes 4325376 | tf_op jit(solution)/shard_map/reshape;reshape | solution.py:170
  338.3 5.3 copy.229
  343.6 5.8 reshape.757
  349.3 4.2 gather_fusion.1
  353.5 4.0 broadcast_select_fusion.2
  357.5 6.1 all-to-all-start
  365.6 4.6 collective-permute-start.6
  374.5 28.3 %collective-permute-done.7 = bf16[3,176,384]{2,1,0:T(8,128)(2,1)S(1)} collective-permute-done((bf16[3,176,384]{2,1,0:T(8,128)(2,1)S(1)}, bf16[3,176,384]{2,1,0:T(8,128)(2,1)S(1)}, u32[]{:S(2)}, u32[]{:S(2)}) %collective-permute-start.7) | collective-permute-done | bytes 405536 | tf_op jit(solution)/shard_map/ppermute | solution.py:21
  408.7 12.4 %maximum_maximum_fusion.1 = (bf16[22,179,384]{2,0,1:T(8,128)(2,1)S(1)}, bf16[22,179,384]{2,0,1:T(8,128)(2,1)}) fusion(bf16[3,176,384]{2,0,1:T(4,128)(2,1)} %copy-done.16, bf16[16,176,384]{2,0,1:T(8,128)(2,1)} %bitcast.131, bf16[3,176,384]{2,0,1:T(4,128)(2,1)} %copy-done.17, bf16[22,3,384]{2,0,1:T(8,128)(2,1)S(1)} %fusion.139, ...), kind=kLoop, calls=%fused_computation.252 | loop fusion | flops 27219456 | bytes 9174528 | tf_op jit(solution)/shard_map/concatenate | solution.py:230
  432.6 63.9 %select_convert_fusion = bf16[16,176,384]{2,0,1:T(8,128)(2,1)S(1)} fusion(bf16[16,176,384]{2,0,1:T(8,128)(2,1)} %bitcast.132, bf16[3,176,384]{2,0,1:T(4,128)(2,1)} %copy-done.16, bf16[3,176,384]{2,0,1:T(4,128)(2,1)} %copy-done.17, bf16[22,179,384]{2,0,1:T(8,128)(2,1)} %get-tuple-element.205, bf16[22,179,384]{2,0,1:T(8,128)(2,1)S(1)} %get-tuple-element.204, ...), kind=kLoop, calls=%fused_computation.228 | loop fusion | flops 179503104 | bytes 96044720 | tf_op jit(solution)/shard_map/convert_element_type | solution.py:233
  504.2 4.0 reshape.761
  508.2 94.6 %all-reduce.3.cloned.1.call-done = f32[1565,384]{0,1:T(8,128)} async-done(((f32[1565,384]{0,1:T(8,128)}), f32[1565,384]{0,1:T(8,128)}) %all-reduce.3.cloned.1.call-update) | async-done | bytes 2403856 | tf_op jit(solution)/shard_map/psum | solution.py:253
  (419 shorter events, 125.9 us)
Async XLA Ops:
  7.2 79.6 %copy-start = (bf16[14,1,16,3072]{3,2,1,0:T(8,128)(2,1)S(1)}, bf16[14,1,16,3072]{3,2,1,0:T(8,128)(2,1)}, u32[]{:S(2)}) copy-start(bf16[14,1,16,3072]{3,2,1,0:T(8,128)(2,1)} %param.13) | copy-start | bytes 4128772
  9.7 117.9 %collective-permute-start.3 = (f32[10944]{0:T(1024)}, f32[10944]{0:T(1024)}, u32[]{:S(2)}, u32[]{:S(2)}) collective-permute-start(f32[10944]{0:T(1024)} %concatenate.143), channel_id=1, source_target_pairs={{0,1},{1,0},{2,3},{3,2},{4,5},{5,4},{6,7},{7,6},{8,9},{9,8},{10,11... | collective-permute-start | bytes 131336 | tf_op jit(solution)/shard_map/ppermute | solution.py:13
  12.2 124.5 %collective-permute-start.5 = (bf16[768,384]{0,1:T(8,128)(2,1)}, bf16[768,384]{0,1:T(8,128)(2,1)}, u32[]{:S(2)}, u32[]{:S(2)}) collective-permute-start(bf16[768,384]{0,1:T(8,128)(2,1)} %copy.227), channel_id=1, source_target_pairs={{0,1},{1,0},{2,3},{3,2},{4,5},{5,4},{6,7},{7,6},{8,9},{9,8},{10,11... | collective-permute-start | bytes 1769480 | tf_op jit(solution)/shard_map/ppermute | solution.py:13
  12.3 123.3 %collective-permute-start.4 = (bf16[384,768]{1,0:T(8,128)(2,1)}, bf16[384,768]{1,0:T(8,128)(2,1)}, u32[]{:S(2)}, u32[]{:S(2)}) collective-permute-start(bf16[384,768]{1,0:T(8,128)(2,1)} %param.17), channel_id=1, source_target_pairs={{0,1},{1,0},{2,3},{3,2},{4,5},{5,4},{6,7},{7,6},{8,9},{9,8},{10,11... | collective-permute-start | bytes 1769480 | tf_op jit(solution)/shard_map/ppermute | solution.py:13
  24.1 79.4 %collective-permute-start.1 = (bf16[3,352,192]{1,2,0:T(8,128)(2,1)}, bf16[3,352,192]{1,2,0:T(8,128)(2,1)}, u32[]{:S(2)}, u32[]{:S(2)}) collective-permute-start(bf16[3,352,192]{1,2,0:T(8,128)(2,1)} %copy.214), channel_id=1, source_target_pairs={{2,0},{4,2},{6,4},{8,6},{10,8},{12,10},{14,12},{16,14},{18,16},{20... | collective-permute-start | bytes 1216520 | tf_op jit(solution)/shard_map/ppermute | solution.py:21
  26.4 79.2 %collective-permute-start = (bf16[3,352,192]{1,2,0:T(8,128)(2,1)}, bf16[3,352,192]{1,2,0:T(8,128)(2,1)}, u32[]{:S(2)}, u32[]{:S(2)}) collective-permute-start(bf16[3,352,192]{1,2,0:T(8,128)(2,1)} %copy.212), channel_id=1, source_target_pairs={{0,2},{2,4},{4,6},{6,8},{8,10},{10,12},{12,14},{14,16},{16,18},{18... | collective-permute-start | bytes 1216520 | tf_op jit(solution)/shard_map/ppermute | solution.py:20
  93.2 118.6 %all-to-all-start.1 = ((bf16[32,16,3072]{2,1,0:T(8,128)(2,1)}), bf16[32,16,3072]{2,1,0:T(8,128)(2,1)}, u32[]{:S(2)}, u32[]{:S(2)}) async-start(bf16[32,16,3072]{2,1,0:T(8,128)(2,1)} %broadcast_select_fusion.1), calls=%async_computation.1 | async-start | bytes 6291456 | tf_op jit(solution)/shard_map/all_to_all | solution.py:116
  124.6 18.1 %copy-start.8 = (bf16[22,182,192]{2,0,1:T(8,128)(2,1)}, bf16[22,182,192]{2,0,1:T(8,128)(2,1)S(1)}, u32[]{:S(2)}) copy-start(bf16[22,182,192]{2,0,1:T(8,128)(2,1)S(1)} %get-tuple-element.199) | copy-start | bytes 4612612
  126.3 14.3 %collective-permute-start.2 = (bf16[22,182,192]{2,1,0:T(8,128)(2,1)}, bf16[22,182,192]{2,1,0:T(8,128)(2,1)}, u32[]{:S(2)}, u32[]{:S(2)}) collective-permute-start(bf16[22,182,192]{2,1,0:T(8,128)(2,1)} %copy.217), channel_id=1, source_target_pairs={{0,1},{1,0},{2,3},{3,2},{4,5},{5,4},{6,7},{7,6},{8,9},{9,8},{10,11... | collective-permute-start | bytes 4612616 | tf_op jit(solution)/shard_map/ppermute | solution.py:13
  130.7 17.2 %copy-start.31 = (f32[384]{0:T(512)}, f32[384]{0:T(512)S(1)}, u32[]{:S(2)}) copy-start(f32[384]{0:T(512)S(1)} %get-tuple-element.186) | copy-start | bytes 4612
  130.7 17.2 %copy-start.33 = (f32[384]{0:T(512)}, f32[384]{0:T(512)S(1)}, u32[]{:S(2)}) copy-start(f32[384]{0:T(512)S(1)} %get-tuple-element.187) | copy-start | bytes 4612
  130.7 17.2 %copy-start.35 = (f32[384]{0:T(512)}, f32[384]{0:T(512)S(1)}, u32[]{:S(2)}) copy-start(f32[384]{0:T(512)S(1)} %get-tuple-element.188) | copy-start | bytes 4612
  130.7 17.2 %copy-start.37 = (f32[384]{0:T(512)}, f32[384]{0:T(512)S(1)}, u32[]{:S(2)}) copy-start(f32[384]{0:T(512)S(1)} %get-tuple-element.189) | copy-start | bytes 4612
  130.8 17.1 %copy-start.41 = (f32[384]{0:T(512)}, f32[384]{0:T(512)S(1)}, u32[]{:S(2)}) copy-start(f32[384]{0:T(512)S(1)} %get-tuple-element.178) | copy-start | bytes 4612
  130.8 17.1 %copy-start.43 = (f32[384]{0:T(512)}, f32[384]{0:T(512)S(1)}, u32[]{:S(2)}) copy-start(f32[384]{0:T(512)S(1)} %get-tuple-element.179) | copy-start | bytes 4612
  130.9 17.1 %copy-start.45 = (f32[384]{0:T(512)}, f32[384]{0:T(512)S(1)}, u32[]{:S(2)}) copy-start(f32[384]{0:T(512)S(1)} %get-tuple-element.180) | copy-start | bytes 4612
  130.9 17.1 %copy-start.47 = (f32[384]{0:T(512)}, f32[384]{0:T(512)S(1)}, u32[]{:S(2)}) copy-start(f32[384]{0:T(512)S(1)} %get-tuple-element.181) | copy-start | bytes 4612
  147.9 36.3 %copy-start.2 = (bf16[22,17,16,384]{3,0,1,2:T(8,128)(2,1)}, bf16[22,17,16,384]{3,0,1,2:T(8,128)(2,1)S(1)}, u32[]{:S(2)}) copy-start(bf16[22,17,16,384]{3,0,1,2:T(8,128)(2,1)S(1)} %maximum_maximum_fusion) | copy-start | bytes 13787140
  250.9 32.5 %slice-start.2 = ((s8[4325376]{0:T(1024)(128)(4,1)}), s8[4194304]{0:T(1024)(128)(4,1)S(1)}, s32[]{:S(2)}) async-start(s8[4325376]{0:T(1024)(128)(4,1)} %bitcast.133), calls=%async_computation.5 | async-start | bytes 8388608
  259.5 18.7 %copy-start.11 = (bf16[2816,384]{1,0:T(8,128)(2,1)S(1)}, bf16[2816,384]{1,0:T(8,128)(2,1)}, u32[]{:S(2)}) copy-start(bf16[2816,384]{1,0:T(8,128)(2,1)} %copy-done.10) | copy-start | bytes 6488068
  259.5 23.9 %slice-start.3 = ((s8[4325376]{0:T(1024)(128)(4,1)}), s8[131072]{0:T(1024)(128)(4,1)S(1)}, s32[]{:S(2)}) async-start(s8[4325376]{0:T(1024)(128)(4,1)} %bitcast.133), calls=%async_computation.6 | async-start | bytes 262144
  327.3 79.7 %copy-start.5 = (bf16[16,11,16,384]{3,0,1,2:T(8,128)(2,1)}, bf16[16,11,16,384]{3,0,1,2:T(8,128)(2,1)S(1)}, u32[]{:S(2)}) copy-start(bf16[16,11,16,384]{3,0,1,2:T(8,128)(2,1)S(1)} %copy.314) | copy-start | bytes 6488068
  330.5 76.7 %collective-permute-start.12 = (f32[10944]{0:T(1024)S(1)}, f32[10944]{0:T(1024)S(1)}, u32[]{:S(2)}, u32[]{:S(2)}) collective-permute-start(f32[10944]{0:T(1024)S(1)} %pad_maximum_fusion.10), channel_id=1, source_target_pairs={{0,1},{1,0},{2,3},{3,2},{4,5},{5,4},{6,7},{7,6},{8,9},{9,8},{10,11... | collective-permute-start | bytes 131336 | tf_op jit(solution)/shard_map/ppermute | solution.py:13
  357.5 255.6 %all-to-all-start = ((bf16[32,16,3072]{2,1,0:T(8,128)(2,1)}), bf16[32,16,3072]{2,1,0:T(8,128)(2,1)}, u32[]{:S(2)}, u32[]{:S(2)}) async-start(bf16[32,16,3072]{2,1,0:T(8,128)(2,1)} %broadcast_select_fusion.2), calls=%async_computation | async-start | bytes 6291456 | tf_op jit(solution)/shard_map/all_to_all | solution.py:180
  363.6 239.2 %all-reduce.3.cloned.1.call-start = ((), (), s32[]{:S(2)}) async-start(), calls=%async_computation.2 | async-start | bytes 5111808 | tf_op jit(solution)/shard_map/psum | solution.py:253
  364.2 38.7 %collective-permute-start.7 = (bf16[3,176,384]{2,1,0:T(8,128)(2,1)S(1)}, bf16[3,176,384]{2,1,0:T(8,128)(2,1)S(1)}, u32[]{:S(2)}, u32[]{:S(2)}) collective-permute-start(bf16[3,176,384]{2,1,0:T(8,128)(2,1)S(1)} %copy.255), channel_id=1, source_target_pairs={{2,0},{4,2},{6,4},{8,6},{10,8},{12,10},{14,12},{16,14},{18,16},{20... | collective-permute-start | bytes 1216520 | tf_op jit(solution)/shard_map/ppermute | solution.py:21
  365.6 41.2 %collective-permute-start.6 = (bf16[3,176,384]{2,1,0:T(8,128)(2,1)S(1)}, bf16[3,176,384]{2,1,0:T(8,128)(2,1)S(1)}, u32[]{:S(2)}, u32[]{:S(2)}) collective-permute-start(bf16[3,176,384]{2,1,0:T(8,128)(2,1)S(1)} %copy.254), channel_id=1, source_target_pairs={{0,2},{2,4},{4,6},{6,8},{8,10},{10,12},{12,14},{14,16},{16,18},{18... | collective-permute-start | bytes 1216520 | tf_op jit(solution)/shard_map/ppermute | solution.py:20
  371.9 49.3 %collective-permute-start.11 = (f32[384,768]{1,0:T(8,128)}, f32[384,768]{1,0:T(8,128)}, u32[]{:S(2)}, u32[]{:S(2)}) collective-permute-start(f32[384,768]{1,0:T(8,128)} %slice.1138), channel_id=1, source_target_pairs={{0,1},{1,0},{2,3},{3,2},{4,5},{5,4},{6,7},{7,6},{8,9},{9,8},{10,11... | collective-permute-start | bytes 3538952 | tf_op jit(solution)/shard_map/ppermute | solution.py:13
  373.3 33.8 %copy-start.15 = (f32[1536,384]{0,1:T(8,128)}, f32[1536,384]{0,1:T(8,128)S(1)}, u32[]{:S(2)}) copy-start(f32[1536,384]{0,1:T(8,128)S(1)} %maximum_select_fusion.1) | copy-start | bytes 7077892
  374.5 54.2 %collective-permute-start.10 = (f32[768,384]{0,1:T(8,128)}, f32[768,384]{0,1:T(8,128)}, u32[]{:S(2)}, u32[]{:S(2)}) collective-permute-start(f32[768,384]{0,1:T(8,128)} %slice.1134), channel_id=1, source_target_pairs={{0,1},{1,0},{2,3},{3,2},{4,5},{5,4},{6,7},{7,6},{8,9},{9,8},{10,11... | collective-permute-start | bytes 3538952 | tf_op jit(solution)/shard_map/ppermute | solution.py:13
  407.2 1.4 collective-permute-start.8
  498.4 3.4 collective-permute-start.9
  (80 other events, 682.3 us)
Sparse Core Ops, SparseCore 0:
  432.6 170.0 all-reduce.2
